TPU v7x, 32 devices: a whole 2x2x4 slice. The times are simulated.
32 devices in a mesh: lon: 8 (over z, core), lat: 4 (over y, x).
Axes of the slice: x: 2, y: 2, z: 4, core: 2. Of those that a mesh axis runs over, the one named last changes fastest.
Arguments:
- sample_collection: float32 [17, 6, 32, 1024], P(None, None, 'lat', 'lon'), may hold values from -5.5 to 5.5
- obs_index: int32 [4, 8, 128], P('lat', 'lon'), may hold values from 0 to 1023, as said below
- obs_count: int32 [4, 8], P('lat', 'lon'), may hold values from 42 to 128
- obs_value: float32 [4, 8, 128], P('lat', 'lon'), may hold values from -5 to 5
- obs_weight: float32 [4, 8, 128], P('lat', 'lon'), may hold values from 8 to 128
Outputs:
- analysis: float32 [17, 6, 32, 1024], P(None, None, 'lat', 'lon')
- analysis_spread: float32 [17, 17], replicated
Inputs may be any that keep to these rules, and one draw needn't show every extreme that they name: `obs_index`: cell number within the tile, row-major over its 8 x 128 cells; slots at or past the tile's count are ignored.
All inputs are finite; a program needn't handle non-finite values.
Results may differ from a plain program's by a relative error of at most 0.00021.
Values sent between devices are 32-bit elements; how exact they have to be, the bound alone decides.
A program may use at most 64 MiB of HBM per device.

v0:
```python
import math

import jax
import jax.numpy as jnp
from jax import lax
from jax.sharding import PartitionSpec as P

UNCERTAINTY_DIRS = 16
MEMBERS = 17
FIELDS = 6
SUBSTEPS = 4


time_step = 0.15
coriolis_scale = 0.5
grav_low = 0.5
depth_top = 4.0
depth_low = 6.0
forget = 0.9
highest = lax.Precision.HIGHEST


def padded_2(shard, sides, width, wrap):
    for axis, dim in sides:
        devices, length = (lax.axis_size(axis), shard.shape[dim])
        up = [(i, (i + 1) % devices) for i in range(devices if wrap else devices - 1)]
        down = [(j, i) for i, j in up]
        last = lax.slice_in_dim(shard, length - width, length, axis=dim)
        leading = lax.slice_in_dim(shard, 0, width, axis=dim)
        before = lax.ppermute(last, axis, up)
        after = lax.ppermute(leading, axis, down)
        shard = jnp.concatenate([before, shard, after], axis=dim)
    return shard


def from_east(quantity):
    return quantity[..., 1:-1, 2:]


def from_west(quantity):
    return quantity[..., 1:-1, :-2]


def from_north(quantity):
    return quantity[..., 2:, 1:-1]


def from_south(quantity):
    return quantity[..., :-2, 1:-1]


def neighbour_mean(quantity):
    return 0.25 * (
        from_east(quantity) + from_west(quantity) + from_north(quantity) + from_south(quantity)
    )


def zonal_slope(quantity):
    return 0.5 * (from_east(quantity) - from_west(quantity))


def merid_slope(quantity):
    return 0.5 * (from_north(quantity) - from_south(quantity))


def layer_update(thick, zonal, merid, pressure, rest_depth, coriolis):
    column = rest_depth + thick
    thick_new = neighbour_mean(thick) - time_step * (
        zonal_slope(column * zonal) + merid_slope(column * merid)
    )
    zonal_here = zonal[..., 1:-1, 1:-1]
    merid_here = merid[..., 1:-1, 1:-1]
    zonal_new = neighbour_mean(zonal) - time_step * (
        zonal_here * zonal_slope(zonal)
        + merid_here * merid_slope(zonal)
        - coriolis * merid_here
        + zonal_slope(pressure)
    )
    merid_new = neighbour_mean(merid) - time_step * (
        zonal_here * zonal_slope(merid)
        + merid_here * merid_slope(merid)
        + coriolis * zonal_here
        + merid_slope(pressure)
    )
    return (thick_new, zonal_new, merid_new)


def advance(padded, coriolis):
    thick_top = padded[..., 0, :, :]
    thick_low = padded[..., 3, :, :]
    press_top = thick_top + thick_low
    press_low = press_top + grav_low * thick_low
    upper_layer = layer_update(
        thick_top, padded[..., 1, :, :], padded[..., 2, :, :], press_top, depth_top, coriolis
    )
    lower_layer = layer_update(
        thick_low, padded[..., 4, :, :], padded[..., 5, :, :], press_low, depth_low, coriolis
    )
    return jnp.stack(upper_layer + lower_layer, axis=-3)


def coriolis_rows(first_row, row_count, total_rows):
    row_values = first_row + jnp.arange(row_count, dtype=jnp.float32)
    return (coriolis_scale * (2.0 * (row_values + 0.5) / total_rows - 1.0)).reshape(row_count, 1)


def margin_steps(padded, rim, first_row, rows_here, total_rows):
    state = padded
    margin = rim - 1
    start = first_row - margin
    count = rows_here + 2 * margin
    state = advance(state, coriolis_rows(start.astype(jnp.float32), count, total_rows))
    return state


def cholesky_lower(matrix):
    order = matrix.shape[0]
    columns = []
    for pivot in range(order):
        partial_col = matrix[:, pivot]
        for earlier in range(pivot):
            partial_col = partial_col - columns[earlier] * columns[earlier][pivot]
        diagonal_root = jnp.sqrt(partial_col[pivot])
        row_mask = (jnp.arange(order) >= pivot).astype(jnp.float32)
        columns.append(partial_col / diagonal_root * row_mask)
    return jnp.stack(columns, axis=1)


def lower_solve(factor, right):
    order = factor.shape[0]
    solved = []
    for row in range(order):
        value = right[row]
        for earlier in range(row):
            value = value - factor[row, earlier] * solved[earlier]
        solved.append(value / factor[row, row])
    return jnp.stack(solved, axis=0)


def upper_solve_transposed(factor, right):
    order = factor.shape[0]
    solved = [None] * order
    for row in range(order - 1, -1, -1):
        value = right[row]
        for later in range(row + 1, order):
            value = value - factor[later, row] * solved[later]
        solved[row] = value / factor[row, row]
    return jnp.stack(solved, axis=0)


def mode_space(obs_gram, obs_proj):
    identity = jnp.eye(UNCERTAINTY_DIRS, dtype=jnp.float32)
    gamma_matrix = identity - 1.0 / MEMBERS
    precision = UNCERTAINTY_DIRS / forget * gamma_matrix + obs_gram
    factor = cholesky_lower(precision)
    weights = upper_solve_transposed(factor, lower_solve(factor, obs_proj))
    projector = (
        jnp.concatenate([identity, jnp.zeros((1, UNCERTAINTY_DIRS), jnp.float32)], axis=0)
        - 1.0 / MEMBERS
    )
    root_fix = identity + (math.sqrt(MEMBERS) - 1.0) / UNCERTAINTY_DIRS
    omega_matrix = jnp.dot(projector, root_fix, precision=highest)
    rotation = math.sqrt(UNCERTAINTY_DIRS) * upper_solve_transposed(factor, omega_matrix.T)
    return (weights, rotation)


def on_device(sample_collection, obs_index, obs_count, obs_value, obs_weight):
    lat_tiles = lax.axis_size("lat")
    lon_tiles = lax.axis_size("lon")
    rows_here = sample_collection.shape[2]
    columns_here = sample_collection.shape[3]
    total_rows = rows_here * lat_tiles
    total_columns = columns_here * lon_tiles
    first_row = lax.axis_index("lat") * rows_here
    members_now = sample_collection
    for substep in range(SUBSTEPS):
        lat_padded = padded_2(members_now, (("lat", 2),), 1, False)
        all_padded = padded_2(lat_padded, (("lon", 3),), 1, True)
        members_now = margin_steps(all_padded, 1, first_row, rows_here, total_rows)
    sample_average_vector = jnp.mean(members_now, axis=0)
    mode_flat = (members_now[:UNCERTAINTY_DIRS] - sample_average_vector).reshape(
        UNCERTAINTY_DIRS, -1
    )
    interface_elevation = (members_now[:, 0] + members_now[:, 3]).reshape(MEMBERS, -1)
    slot_cells = obs_index.reshape(-1)
    slot_total = slot_cells.shape[0]
    cell_numbers = jnp.arange(rows_here * columns_here, dtype=jnp.int32)
    selector = (slot_cells[:, None] == cell_numbers[None, :]).astype(jnp.float32)
    observed = lax.dot_general(
        interface_elevation, selector, (((1,), (1,)), ((), ())), precision=highest
    )
    live_slots = (jnp.arange(slot_total, dtype=jnp.int32) < obs_count.reshape(())).astype(
        jnp.float32
    )
    weight = obs_weight.reshape(-1) * live_slots / (slot_total * lat_tiles * lon_tiles)
    obs_mean = jnp.mean(observed, axis=0)
    anomaly = observed[:UNCERTAINTY_DIRS] - obs_mean
    innovation = obs_value.reshape(-1) - obs_mean
    weighted = anomaly * weight
    gram_local = jnp.dot(weighted, anomaly.T, precision=highest)
    proj_local = jnp.dot(weighted, innovation, precision=highest)
    cell_total = FIELDS * total_rows * total_columns
    mode_local = jnp.dot(mode_flat, mode_flat.T, precision=highest)
    obs_gram, obs_proj, mode_gram = lax.psum((gram_local, proj_local, mode_local), ("lon", "lat"))
    weights, rotation = mode_space(obs_gram, obs_proj)
    spread = (
        jnp.dot(rotation.T, jnp.dot(mode_gram, rotation, precision=highest), precision=highest)
        / cell_total
    )
    coefficient = weights[:, None] + rotation
    update = jnp.dot(coefficient.T, mode_flat, precision=highest).reshape(members_now.shape)
    analysis = sample_average_vector + update
    return (analysis, spread)


def solution(mesh):
    return jax.shard_map(
        on_device,
        mesh=mesh,
        in_specs=(
            P(None, None, "lat", "lon"),
            P("lat", "lon", None),
            P("lat", "lon"),
            P("lat", "lon", None),
            P("lat", "lon", None),
        ),
        out_specs=(P(None, None, "lat", "lon"), P()),
        check_vma=False,
    )
```

profile of v0, /device:TPU:0, one launch (start us, length us, event | category | flops | bytes accessed | tf_op | source)
XLA Modules:
  0.0 555.6 jit_solution(6147046531127155356)
XLA Ops:
  1.9 4.8 collective-permute-start
  6.8 1.3 collective-permute-start.1
  9.9 3.2 collective-permute-done.1
  14.5 3.5 collective-permute-start.3
  22.6 4.3 collective-permute-start.4
  26.9 1.3 collective-permute-start.5
  28.9 4.3 collective-permute-done.5
  34.4 3.6 collective-permute-start.7
  42.5 3.4 collective-permute-start.8
  47.8 4.3 collective-permute-done.9
  53.4 3.6 collective-permute-start.11
  61.5 3.1 collective-permute-start.12
  66.5 4.3 collective-permute-done.13
  72.1 3.7 collective-permute-start.15
  82.0 38.4 %all-reduce.1 = (f32[16,16]{1,0:T(8,128)S(1)}, f32[16]{0:T(128)S(1)}, f32[16,16]{1,0:T(8,128)S(1)}) all-reduce(f32[16,16]{1,0:T(8,128)S(1)} %fusion.146, f32[16]{0:T(128)S(1)} %convolution_bitcast_fusion.1, f32[16,16]{1,0:T(8,128)S(1)} %convolution_bitcast_fusion), channel_id=1, replica_groups=mesh['lon'=8,'lat'=4] {'lon','lat'}, use_global_device_ids=true, to_apply=%region_3.0 | all-reduce | flops 528 | bytes 4224 | tf_op jit(solution)/shard_map/psum | solution.py:204
  127.5 4.1 fusion.158
  137.3 5.9 %fusion.149 = (f32[16]{0:T(128)S(1)}, f32[16]{0:T(128)S(1)}, f32[16]{0:T(128)S(1)}, f32[16]{0:T(128)S(1)}, f32[16]{0:T(128)S(1)}, /*index=5*/f32[16]{0:T(128)S(1)}, f32[16]{0:T(128)S(1)}, f32[16]{0:T(128)S(1)}, f32[16]{0:T(128)S(1)}) fusion(f32[16,16]{1,0:T(8,128)S(1)} %multiply_add_fusion.4, f32[]{:T(128)} %bitcast.206, f32[]{:T(128)} %bitcast.189, ...), kind=kLoop, calls=%fused_computation.270 | loop fusion | flops 304 | bytes 1256 | tf_op jit(solution)/shard_map/sub | solution.py:122
  157.2 1.8 multiply_subtract_fusion.11
  164.7 2.6 multiply_subtract_fusion.10
  173.9 3.2 multiply_subtract_fusion.9
  184.2 3.7 multiply_subtract_fusion.8
  195.6 4.3 multiply_subtract_fusion.7
  208.3 5.0 multiply_subtract_fusion.6
  222.1 5.7 %multiply_subtract_fusion.5 = f32[16]{0:T(128)S(1)} fusion(f32[16]{0:T(128)S(1)} %get-tuple-element.17, f32[]{:T(128)} %bitcast.129, f32[]{:T(128)} %bitcast.139, f32[]{:T(128)} %bitcast.138, f32[]{:T(128)} %bitcast.137, f32[]{:T(128)} %bitcast.136, f32[]{:T(128)} %bitcast.135, f32[]{:T(128)} %bitcast.134, f32[]{:T(128)} %bitcast.133, f32[]{:T(128)} %bitcast.132, ...), kind=kLoop, calls=%fused_computation.461 | loop fusion | flops 704 | bytes 772 | tf_op jit(solution)/shard_map/sub | solution.py:122
  237.4 6.4 %multiply_subtract_fusion.4 = f32[16]{0:T(128)S(1)} fusion(f32[16]{0:T(128)S(1)} %get-tuple-element.16, f32[]{:T(128)} %bitcast.142, f32[]{:T(128)} %bitcast.153, f32[]{:T(128)} %bitcast.152, f32[]{:T(128)} %bitcast.151, f32[]{:T(128)} %bitcast.150, f32[]{:T(128)} %bitcast.149, f32[]{:T(128)} %bitcast.148, f32[]{:T(128)} %bitcast.147, f32[]{:T(128)} %bitcast.146, ...), kind=kLoop, calls=%fused_computation.460 | loop fusion | flops 784 | bytes 844 | tf_op jit(solution)/shard_map/sub | solution.py:122
  253.8 6.7 %multiply_subtract_fusion.3 = f32[16]{0:T(128)S(1)} fusion(f32[16]{0:T(128)S(1)} %get-tuple-element.15, f32[]{:T(128)} %bitcast.156, f32[]{:T(128)} %bitcast.168, f32[]{:T(128)} %bitcast.167, f32[]{:T(128)} %bitcast.166, f32[]{:T(128)} %bitcast.165, f32[]{:T(128)} %bitcast.164, f32[]{:T(128)} %bitcast.163, f32[]{:T(128)} %bitcast.162, f32[]{:T(128)} %bitcast.161, ...), kind=kLoop, calls=%fused_computation.459 | loop fusion | flops 864 | bytes 916 | tf_op jit(solution)/shard_map/sub | solution.py:122
  271.3 7.6 %multiply_subtract_fusion.2 = f32[16]{0:T(128)S(1)} fusion(f32[16]{0:T(128)S(1)} %get-tuple-element.14, f32[]{:T(128)} %bitcast.171, f32[]{:T(128)} %bitcast.184, f32[]{:T(128)} %bitcast.183, f32[]{:T(128)} %bitcast.182, f32[]{:T(128)} %bitcast.181, f32[]{:T(128)} %bitcast.180, f32[]{:T(128)} %bitcast.179, f32[]{:T(128)} %bitcast.178, f32[]{:T(128)} %bitcast.177, ...), kind=kLoop, calls=%fused_computation.458 | loop fusion | flops 944 | bytes 988 | tf_op jit(solution)/shard_map/sub | solution.py:122
  290.3 8.1 %multiply_subtract_fusion.1 = f32[16]{0:T(128)S(1)} fusion(f32[16]{0:T(128)S(1)} %get-tuple-element.13, f32[]{:T(128)} %bitcast.187, f32[]{:T(128)} %bitcast.201, f32[]{:T(128)} %bitcast.200, f32[]{:T(128)} %bitcast.199, f32[]{:T(128)} %bitcast.198, f32[]{:T(128)} %bitcast.197, f32[]{:T(128)} %bitcast.196, f32[]{:T(128)} %bitcast.195, f32[]{:T(128)} %bitcast.194, ...), kind=kLoop, calls=%fused_computation.457 | loop fusion | flops 1024 | bytes 1060 | tf_op jit(solution)/shard_map/sub | solution.py:122
  310.2 8.5 %multiply_subtract_fusion = f32[16]{0:T(128)S(1)} fusion(f32[16]{0:T(128)S(1)} %get-tuple-element.12, f32[]{:T(128)} %bitcast.204, f32[]{:T(128)} %bitcast.219, f32[]{:T(128)} %bitcast.218, f32[]{:T(128)} %bitcast.217, f32[]{:T(128)} %bitcast.216, f32[]{:T(128)} %bitcast.215, f32[]{:T(128)} %bitcast.214, f32[]{:T(128)} %bitcast.213, f32[]{:T(128)} %bitcast.212, ...), kind=kLoop, calls=%fused_computation.456 | loop fusion | flops 1104 | bytes 1132 | tf_op jit(solution)/shard_map/sub | solution.py:122
  407.8 65.3 %subtract_divide_fusion = (f32[1,17]{1,0:T(1,128)S(1)}, f32[1,17]{1,0:T(1,128)S(1)}, f32[1,17]{1,0:T(1,128)S(1)}, f32[1,17]{1,0:T(1,128)S(1)}, f32[1,17]{1,0:T(1...) fusion(f32[16,17]{1,0:T(8,128)S(1)} %fusion.143, ...), kind=kLoop, calls=%fused_computation.446 | loop fusion | flops 3332 | bytes 2392 | tf_op jit(solution)/shard_map/div | solution.py:147
  473.1 57.9 %fusion.195 = (f32[17]{0:T(128)S(1)}, f32[17]{0:T(128)S(1)}, f32[17]{0:T(128)S(1)}, f32[17]{0:T(128)S(1)}, f32[17]{0:T(128)S(1)}, /*index=5*/f32[17]{0:T(128)S(1...) fusion(f32[16,17]{1,0:T(8,128)S(1)} %fusion.143, f32[1,17]{1,0:T(1,128)S(1)} %get-tuple-element.40, ...), kind=kLoop, calls=%fused_computation.367 | loop fusion | flops 2992 | bytes 2004 | tf_op jit(solution)/shard_map/div | solution.py:147
  531.0 19.5 %fusion.229 = (f32[1,17]{1,0:T(1,128)S(1)}, f32[17]{0:T(128)S(1)}) fusion(f32[1,17]{1,0:T(1,128)S(1)} %get-tuple-element.43, f32[1,17]{1,0:T(1,128)S(1)} %get-tuple-element.42, f32[1,17]{1,0:T(1,128)S(1)} %get-tuple-element.41, f32[1,17]{1,0:T(1,128)S(1)} %get-tuple-element.40, f32[17]{0:T(128)S(1)} %get-tuple-element.55, f32[17]{0:T(128)S(1)} %get-tuple-element.54, ...), kind=kLoop, calls=%fused_computation.473 | loop fusion | flops 1020 | bytes 1348 | tf_op jit(solution)/shard_map/stack | solution.py:148
  (169 shorter events, 57.9 us)
Async XLA Ops:
  1.9 6.8 %collective-permute-start = (f32[17,6,1,128]{3,0,2,1:T(8,128)S(1)}, f32[17,6,1,128]{3,0,2,1:T(8,128)S(1)}, u32[]{:S(2)}, u32[]{:S(2)}) collective-permute-start(f32[17,6,1,128]{3,0,2,1:T(8,128)S(1)} %copy.88), channel_id=1, source_target_pairs={{0,1},{1,2},{2,3},{4,5},{5,6},{6,7},{8,9},{9,10},{10,11},{12,13},{... | collective-permute-start | bytes 156680 | tf_op jit(solution)/shard_map/ppermute | solution.py:30
  6.8 6.2 %collective-permute-start.1 = (f32[17,6,1,128]{3,0,2,1:T(8,128)S(1)}, f32[17,6,1,128]{3,0,2,1:T(8,128)S(1)}, u32[]{:S(2)}, u32[]{:S(2)}) collective-permute-start(f32[17,6,1,128]{3,0,2,1:T(8,128)S(1)} %copy.89), channel_id=1, source_target_pairs={{1,0},{2,1},{3,2},{5,4},{6,5},{7,6},{9,8},{10,9},{11,10},{13,12},{... | collective-permute-start | bytes 156680 | tf_op jit(solution)/shard_map/ppermute | solution.py:31
  13.9 5.2 collective-permute-start.2
  14.5 5.2 collective-permute-start.3
  22.6 6.3 %collective-permute-start.4 = (f32[17,6,1,128]{3,0,2,1:T(8,128)S(1)}, f32[17,6,1,128]{3,0,2,1:T(8,128)S(1)}, u32[]{:S(2)}, u32[]{:S(2)}) collective-permute-start(f32[17,6,1,128]{3,0,2,1:T(8,128)S(1)} %get-tuple-element.119), channel_id=1, source_target_pairs={{0,1},{1,2},{2,3},{4,5},{5,6},{6,7},{8,9},{9,10},{10,11},{12,13},{... | collective-permute-start | bytes 156680 | tf_op jit(solution)/shard_map/ppermute | solution.py:30
  26.9 6.2 %collective-permute-start.5 = (f32[17,6,1,128]{3,0,2,1:T(8,128)S(1)}, f32[17,6,1,128]{3,0,2,1:T(8,128)S(1)}, u32[]{:S(2)}, u32[]{:S(2)}) collective-permute-start(f32[17,6,1,128]{3,0,2,1:T(8,128)S(1)} %get-tuple-element.120), channel_id=1, source_target_pairs={{1,0},{2,1},{3,2},{5,4},{6,5},{7,6},{9,8},{10,9},{11,10},{13,12},{... | collective-permute-start | bytes 156680 | tf_op jit(solution)/shard_map/ppermute | solution.py:31
  33.9 5.2 collective-permute-start.6
  34.4 5.1 collective-permute-start.7
  42.5 5.4 collective-permute-start.8
  45.9 6.2 %collective-permute-start.9 = (f32[17,6,1,128]{3,0,2,1:T(8,128)S(1)}, f32[17,6,1,128]{3,0,2,1:T(8,128)S(1)}, u32[]{:S(2)}, u32[]{:S(2)}) collective-permute-start(f32[17,6,1,128]{3,0,2,1:T(8,128)S(1)} %get-tuple-element.118), channel_id=1, source_target_pairs={{1,0},{2,1},{3,2},{5,4},{6,5},{7,6},{9,8},{10,9},{11,10},{13,12},{... | collective-permute-start | bytes 156680 | tf_op jit(solution)/shard_map/ppermute | solution.py:31
  52.9 5.2 collective-permute-start.10
  53.4 5.2 collective-permute-start.11
  61.5 5.0 collective-permute-start.12
  64.5 6.2 %collective-permute-start.13 = (f32[17,6,1,128]{3,0,2,1:T(8,128)S(1)}, f32[17,6,1,128]{3,0,2,1:T(8,128)S(1)}, u32[]{:S(2)}, u32[]{:S(2)}) collective-permute-start(f32[17,6,1,128]{3,0,2,1:T(8,128)S(1)} %get-tuple-element.116), channel_id=1, source_target_pairs={{1,0},{2,1},{3,2},{5,4},{6,5},{7,6},{9,8},{10,9},{11,10},{13,12},{... | collective-permute-start | bytes 156680 | tf_op jit(solution)/shard_map/ppermute | solution.py:31
  71.6 5.2 collective-permute-start.14
  72.1 5.3 collective-permute-start.15
  78.8 0.7 copy-start.1
  78.8 1.1 copy-start
  78.8 1.2 copy-start.2
where the time goes:
time: 562 us; the launch traced here: 556 us
  other arithmetic  228 us (41%)
  between operations  194 us (35%)
  blocking collectives  38.4 us (7%)
  starting transfers between devices  35.3 us (6%)
  local copies, waits for them, and re-layouts  34.5 us (6%)
  waiting for transfers between devices  22.3 us (4%)
    div x2, other arithmetic, upper_solve_transposed(): solved[row] = value / factor[row, row]  123 us
    sub x16, other arithmetic, cholesky_lower(): partial_col = partial_col - columns[earlier] * columns[earlier][pivot]  75.4 us
    psum x1, blocking collectives, on_device(): lax.psum((gram_local, proj_local, mode_local), ('lon', 'lat'))  38.4 us
    ppermute x8, starting transfers between devices, padded_2(): after = lax.ppermute(leading, axis, down)  19.6 us
    another operation x1, other arithmetic, upper_solve_transposed(): return jnp.stack(solved, axis=0)  19.5 us
    ppermute x8, waiting for transfers between devices, padded_2(): after = lax.ppermute(leading, axis, down)  16.3 us
    ppermute x8, starting transfers between devices, padded_2(): before = lax.ppermute(last, axis, up)  15.7 us
  transfers between devices with their start and end apart: 16, of which 13 were waited for; matrix products, arithmetic and copies ran while one was open for 1% of the time, Pallas kernels for 0%

commit v1 on v0

v1 whole, which is shorter than its diff:
```python
import functools
import math

import jax
import jax.numpy as jnp
import numpy as np
from jax import lax
from jax.experimental import pallas as pl
from jax.experimental.pallas import tpu as pltpu
from jax.sharding import PartitionSpec as P

SUBSTEPS = 4

time_step = 0.15
coriolis_scale = 0.5
grav_low = 0.5
depth_top = 4.0
depth_low = 6.0
forget = 0.9
highest = lax.Precision.HIGHEST
MESH = pl.DeviceIdType.MESH

SYS = 32


def split2(x):
    high = x.astype(jnp.bfloat16)
    low = (x - high.astype(jnp.float32)).astype(jnp.bfloat16)
    return high, low


def split3(x):
    high = x.astype(jnp.bfloat16)
    rest = x - high.astype(jnp.float32)
    mid = rest.astype(jnp.bfloat16)
    low = (rest - mid.astype(jnp.float32)).astype(jnp.bfloat16)
    return high, mid, low


def dot(a, b):
    return jnp.dot(a, b, preferred_element_type=jnp.float32)


def dot_nt(a, b, precision=None):
    return lax.dot_general(
        a, b, (((1,), (1,)), ((), ())), precision=precision, preferred_element_type=jnp.float32
    )


def kernel(
    dims, x_ref, index_ref, count_ref, value_ref, weight_ref, system_ref, omega_ref,
    out_ref, spread_ref,
    state, send_low, send_high, send_cols, from_north, from_south, from_east, from_west,
    surface, selector, means, modes, parts, gather_lon, gather_lat,
    halo_send, halo_recv, lon_send, lon_recv, lat_send, lat_recv,
):
    members, fields, rows, cols, n_lat, n_lon = dims
    dirs = members - 1
    tiles = members * fields
    cells = rows * cols
    slots = index_ref.shape[1]
    me_lon, me_lat = lax.axis_index("lon"), lax.axis_index("lat")

    def lon_at(d):
        return (lax.rem(me_lon + d + n_lon, n_lon), me_lat)

    def lat_at(d):
        return (me_lon, lax.rem(me_lat + d + n_lat, n_lat))

    partners = [lon_at(d) for d in range(1, n_lon)] + [lat_at(d) for d in range(1, n_lat)]
    barrier = pltpu.get_barrier_semaphore()
    for partner in partners:
        pl.semaphore_signal(barrier, inc=1, device_id=partner, device_id_type=MESH)

    lane = lax.broadcasted_iota(jnp.int32, (rows, cols), 1)
    row = lax.broadcasted_iota(jnp.int32, (rows, cols), 0)
    half = lane // 2
    first_lane, last_lane = lane == 0, lane == cols - 1
    first_row, last_row = row == 0, row == rows - 1
    even_lane = (lane - 2 * half) == 0
    row_number = (row + me_lat * rows).astype(jnp.float32)
    coriolis = coriolis_scale * (2.0 * (row_number + 0.5) / (rows * n_lat) - 1.0)
    turn = time_step * coriolis
    ghost = 0.5 * time_step

    def pack(packed, tile, quantity):
        base = tile - tile % 2
        moved = pltpu.roll(quantity, base + 1, 1)
        packed[tile % 2] = jnp.where(half == base // 2, moved, packed[tile % 2])

    def put_edges(slot, tile, quantity):
        send_low[slot, tile : tile + 1, :] = quantity[0:1, :]
        send_high[slot, tile : tile + 1, :] = quantity[rows - 1 : rows, :]

    def put_cols(slot, packed):
        send_cols[slot, 0:rows, :] = packed[0]
        send_cols[slot, rows : 2 * rows, :] = packed[1]

    packed = [jnp.zeros((rows, cols), jnp.float32)] * 2
    for tile in range(tiles):
        quantity = x_ref[tile * rows : (tile + 1) * rows, :]
        state[0, tile * rows : (tile + 1) * rows, :] = quantity
        put_edges(0, tile, quantity)
        pack(packed, tile, quantity)
    put_cols(0, packed)

    for r in range(rows):
        cell = lax.broadcasted_iota(jnp.int32, (cols, slots), 0) + r * cols
        hit = jnp.where(cell == index_ref[...], 1.0, 0.0)
        selector[r * cols : (r + 1) * cols, :] = hit.astype(jnp.bfloat16)
    live = lax.broadcasted_iota(jnp.int32, (1, slots), 1) < count_ref[...]
    weight = jnp.where(live, weight_ref[...], 0.0) / (slots * n_lat * n_lon)
    surface[...] = jnp.zeros_like(surface)

    pl.semaphore_wait(barrier, len(partners))

    def substep(step, carry):
        now, later = lax.rem(step, 2), lax.rem(step + 1, 2)
        copies = []
        for number, (source, target, device) in enumerate((
            (send_low, from_north, lat_at(-1)),
            (send_high, from_south, lat_at(1)),
            (send_cols, from_east, lon_at(-1)),
            (send_cols, from_west, lon_at(1)),
        )):
            copy = pltpu.make_async_remote_copy(
                src_ref=source.at[step],
                dst_ref=target.at[step],
                send_sem=halo_send.at[step, number],
                recv_sem=halo_recv.at[step, number],
                device_id=device,
                device_id_type=MESH,
            )
            copy.start()
            copies.append(copy)
        for copy in copies:
            copy.wait()
        north_on = jnp.where(me_lat < n_lat - 1, 1.0, 0.0)
        south_on = jnp.where(me_lat > 0, 1.0, 0.0)
        columns = []
        for parity in range(2):
            east = pltpu.roll(from_east[step, parity * rows : (parity + 1) * rows, :], cols - 1, 1)
            west = pltpu.roll(from_west[step, parity * rows : (parity + 1) * rows, :], 1, 1)
            columns.append(jnp.where(even_lane, east, west))

        packed = [jnp.zeros((rows, cols), jnp.float32)] * 2
        for member in range(members):
            here, east, west, north, south = [], [], [], [], []
            for field in range(fields):
                tile = member * fields + field
                base = tile - tile % 2
                q = state[now, tile * rows : (tile + 1) * rows, :]
                side = pltpu.roll(columns[tile % 2], cols - 1 - base, 1)
                above = from_north[step, tile : tile + 1, :] * north_on
                below = from_south[step, tile : tile + 1, :] * south_on
                here.append(q)
                east.append(jnp.where(last_lane, side, pltpu.roll(q, cols - 1, 1)))
                west.append(jnp.where(first_lane, side, pltpu.roll(q, 1, 1)))
                north.append(jnp.where(last_row, above, pltpu.roll(q, rows - 1, 0)))
                south.append(jnp.where(first_row, below, pltpu.roll(q, 1, 0)))
            dx = [e - w for e, w in zip(east, west)]
            dy = [n - s for n, s in zip(north, south)]
            mean = [0.25 * ((e + w) + (n + s)) for e, w, n, s in zip(east, west, north, south)]
            px_top, py_top = dx[0] + dx[3], dy[0] + dy[3]
            px = (px_top, px_top + grav_low * dx[3])
            py = (py_top, py_top + grav_low * dy[3])
            after = []
            for layer, depth in enumerate((depth_top, depth_low)):
                h, u, v = 3 * layer, 3 * layer + 1, 3 * layer + 2
                flux = ((depth + east[h]) * east[u] - (depth + west[h]) * west[u]) + (
                    (depth + north[h]) * north[v] - (depth + south[h]) * south[v]
                )
                after.append(mean[h] - ghost * flux)
                after.append(
                    mean[u]
                    - ghost * (here[u] * dx[u] + here[v] * dy[u] + px[layer])
                    + turn * here[v]
                )
                after.append(
                    mean[v]
                    - ghost * (here[u] * dx[v] + here[v] * dy[v] + py[layer])
                    - turn * here[u]
                )
            for field in range(fields):
                tile = member * fields + field
                state[later, tile * rows : (tile + 1) * rows, :] = after[field]
                put_edges(step + 1, tile, after[field])
                pack(packed, tile, after[field])
            surface[member * rows : (member + 1) * rows, :] = after[0] + after[3]
        put_cols(step + 1, packed)
        return carry

    lax.fori_loop(0, SUBSTEPS, substep, 0)
    final = SUBSTEPS % 2

    pad = surface.shape[0] // rows
    observed = jnp.zeros((3 * pad, slots), jnp.float32)
    for r in range(rows):
        level = surface[pl.ds(r, pad, stride=rows), :]
        observed += dot(
            jnp.concatenate(split3(level), axis=0), selector[r * cols : (r + 1) * cols, :]
        )
    observed = observed[0:pad] + observed[pad : 2 * pad] + observed[2 * pad : 3 * pad]
    obs_mean = jnp.sum(observed, axis=0, keepdims=True) * (1.0 / members)
    anomaly = observed[0:dirs] - obs_mean
    innovation = value_ref[...] - obs_mean
    top = lax.broadcasted_iota(jnp.int32, (8, slots), 0) == 0
    right = jnp.concatenate(
        [jnp.zeros((SYS, slots), jnp.float32), anomaly, jnp.where(top, innovation, 0.0)], axis=0
    )
    gather_lon[me_lon] = jnp.zeros(gather_lon.shape[1:], jnp.float32)
    gather_lon[me_lon, 0:dirs, 0 : right.shape[0]] = dot_nt(anomaly * weight, right, highest)

    for field in range(fields):
        total = state[final, field * rows : (field + 1) * rows, :]
        for member in range(1, members):
            at = (member * fields + field) * rows
            total = total + state[final, at : at + rows, :]
        total = total * (1.0 / members)
        means[field * rows : (field + 1) * rows, :] = total
        for member in range(dirs):
            at = (member * fields + field) * rows
            modes[at : at + rows, :] = state[final, at : at + rows, :] - total
    for line in range(fields * rows):
        high, low = split2(modes[pl.ds(line, dirs, stride=fields * rows), :])
        parts[0:dirs, line * cols : (line + 1) * cols] = high
        parts[dirs : 2 * dirs, line * cols : (line + 1) * cols] = low
    high, low = parts[0:dirs, :], parts[dirs : 2 * dirs, :]
    gather_lon[me_lon, dirs : 2 * dirs, 0:dirs] = (
        dot_nt(high, high) + dot_nt(high, low) + dot_nt(low, high)
    )

    def gather(buffer, me, count, device_of, send, recv):
        copies = []
        for d in range(1, count):
            copy = pltpu.make_async_remote_copy(
                src_ref=buffer.at[me],
                dst_ref=buffer.at[me],
                send_sem=send.at[d],
                recv_sem=recv.at[me],
                device_id=device_of(d),
                device_id_type=MESH,
            )
            copy.start()
            copies.append(copy)
        for d in range(1, count):
            other = lax.rem(me + d, count)
            pltpu.make_async_remote_copy(
                src_ref=buffer.at[other],
                dst_ref=buffer.at[other],
                send_sem=send.at[d],
                recv_sem=recv.at[other],
                device_id=device_of(d),
                device_id_type=MESH,
            ).wait_recv()
        for copy in copies:
            copy.wait_send()
        total = buffer[0]
        for i in range(1, count):
            total = total + buffer[i]
        return total

    gather_lat[me_lat] = gather(gather_lon, me_lon, n_lon, lon_at, lon_send, lon_recv)
    total = gather(gather_lat, me_lat, n_lat, lat_at, lat_send, lat_recv)

    system = total[0:dirs] + system_ref[...]
    mode_gram = total[dirs : 2 * dirs, 0:dirs]
    below = lax.broadcasted_iota(jnp.int32, system.shape, 0)
    across = lax.broadcasted_iota(jnp.int32, system.shape, 1)
    for j in range(dirs):
        pivot = system[j : j + 1, SYS + j : SYS + j + 1]
        column = system[:, SYS + j : SYS + j + 1]
        factor = jnp.where(below > j, column / pivot, 0.0)
        system = system - factor * system[j : j + 1, :]
    diagonal = jnp.sum(jnp.where(across == below + SYS, system, 0.0), axis=1, keepdims=True)
    system = system / jnp.sqrt(diagonal)
    solved = system[:, SYS + dirs : SYS + dirs + 1]
    inverse = system[:, 0:dirs]
    weights = jnp.sum(solved * inverse, axis=0, keepdims=True)
    rotation = jnp.dot(
        omega_ref[...], inverse, precision=highest, preferred_element_type=jnp.float32
    )
    spread = dot_nt(
        jnp.dot(rotation, mode_gram, precision=highest, preferred_element_type=jnp.float32),
        rotation,
        highest,
    )
    spread_ref[...] = spread * (1.0 / (fields * cells * n_lat * n_lon))

    c_high, c_low = split2(rotation + weights)
    for field in range(fields):
        block = pl.ds(field * cells, cells)
        high = parts[0:dirs, block]
        update = dot(c_high, high) + dot(c_high, parts[dirs : 2 * dirs, block]) + dot(c_low, high)
        for r in range(rows):
            line = field * rows + r
            out_ref[pl.ds(line, members, stride=fields * rows), :] = (
                update[:, r * cols : (r + 1) * cols] + means[line : line + 1, :]
            )


def constants(members):
    dirs = members - 1
    identity = np.eye(dirs)
    system = np.zeros((dirs, 128))
    system[:, 0:dirs] = identity
    system[:, SYS : SYS + dirs] = dirs / forget * (identity - 1.0 / members)
    projector = np.concatenate([identity, np.zeros((1, dirs))], axis=0) - 1.0 / members
    omega = projector @ (identity + (math.sqrt(members) - 1.0) / dirs)
    return system.astype(np.float32), (math.sqrt(dirs) * omega).astype(np.float32)


def on_device(n_lat, n_lon, sample_collection, obs_index, obs_count, obs_value, obs_weight):
    members, fields, rows, cols = sample_collection.shape
    slots = obs_index.shape[-1]
    dirs, tiles = members - 1, members * fields
    padded_tiles = -(-tiles // 8) * 8
    pad = -(-members // 16) * 16
    system, omega = constants(members)
    f32 = jnp.float32
    dims = (members, fields, rows, cols, n_lat, n_lon)
    analysis, spread = pl.pallas_call(
        functools.partial(kernel, dims),
        out_shape=(
            jax.ShapeDtypeStruct((tiles * rows, cols), f32),
            jax.ShapeDtypeStruct((members, members), f32),
        ),
        in_specs=[pl.BlockSpec(memory_space=pltpu.VMEM)] * 7,
        out_specs=(pl.BlockSpec(memory_space=pltpu.VMEM),) * 2,
        scratch_shapes=[
            pltpu.VMEM((2, tiles * rows, cols), f32),
            pltpu.VMEM((SUBSTEPS + 1, padded_tiles, cols), f32),
            pltpu.VMEM((SUBSTEPS + 1, padded_tiles, cols), f32),
            pltpu.VMEM((SUBSTEPS + 1, 2 * rows, cols), f32),
            pltpu.VMEM((SUBSTEPS, padded_tiles, cols), f32),
            pltpu.VMEM((SUBSTEPS, padded_tiles, cols), f32),
            pltpu.VMEM((SUBSTEPS, 2 * rows, cols), f32),
            pltpu.VMEM((SUBSTEPS, 2 * rows, cols), f32),
            pltpu.VMEM((pad * rows, cols), f32),
            pltpu.VMEM((rows * cols, slots), jnp.bfloat16),
            pltpu.VMEM((fields * rows, cols), f32),
            pltpu.VMEM((dirs * fields * rows, cols), f32),
            pltpu.VMEM((2 * dirs, fields * rows * cols), jnp.bfloat16),
            pltpu.VMEM((n_lon, 2 * dirs, 128), f32),
            pltpu.VMEM((n_lat, 2 * dirs, 128), f32),
            pltpu.SemaphoreType.DMA((SUBSTEPS, 4)),
            pltpu.SemaphoreType.DMA((SUBSTEPS, 4)),
            pltpu.SemaphoreType.DMA((n_lon,)),
            pltpu.SemaphoreType.DMA((n_lon,)),
            pltpu.SemaphoreType.DMA((n_lat,)),
            pltpu.SemaphoreType.DMA((n_lat,)),
        ],
        compiler_params=pltpu.CompilerParams(
            collective_id=0, has_side_effects=True, vmem_limit_bytes=32 * 1024 * 1024
        ),
    )(
        sample_collection.reshape(tiles * rows, cols),
        obs_index.reshape(1, slots),
        obs_count.reshape(1, 1),
        obs_value.reshape(1, slots),
        obs_weight.reshape(1, slots),
        jnp.asarray(system),
        jnp.asarray(omega),
    )
    return analysis.reshape(sample_collection.shape), spread


def solution(mesh):
    return jax.shard_map(
        functools.partial(on_device, mesh.shape["lat"], mesh.shape["lon"]),
        mesh=mesh,
        in_specs=(
            P(None, None, "lat", "lon"),
            P("lat", "lon", None),
            P("lat", "lon"),
            P("lat", "lon", None),
            P("lat", "lon", None),
        ),
        out_specs=(P(None, None, "lat", "lon"), P()),
        check_vma=False,
    )
```

time: 562 us -> 43.2 us (0.08); the launches traced: 556 us -> 42.9 us
  other arithmetic: 228 us -> 0 us
  between operations: 194 us -> 1.33 us
  blocking collectives: 38.4 us -> 0 us
  Pallas kernels: 0 us -> 37.2 us
  starting transfers between devices: 35.3 us -> 0 us
  local copies, waits for them, and re-layouts: 34.5 us -> 4.38 us
  waiting for transfers between devices: 22.3 us -> 0 us
    div x6 -> x0, other arithmetic: 123 us -> none  [the longest x2 123 us: upper_solve_transposed(): solved[row] = value / factor[row, row]]
    sub x17 -> x0, other arithmetic: 75.4 us -> none  [the longest x16 75.4 us: cholesky_lower(): partial_col = partial_col - columns[earlier] * columns[earlier][pivot]]
    psum x1 -> x0, blocking collectives: 38.4 us -> none  [on_device(): lax.psum((gram_local, proj_local, mode_local), ('lon', 'lat'))]
    pallas_call x0 -> x1, Pallas kernels: none -> 37.2 us  [on_device(): pl.pallas_call(functools.partial(kernel, dims), out_shape=(jax.ShapeDtype...]
    ppermute x16 -> x0, starting transfers between devices: 35.3 us -> none  [the longest x8 19.6 us: padded_2(): after = lax.ppermute(leading, axis, down)]
    slice x49 -> x0, local copies, waits for them, and re-layouts: 27.5 us -> none  [the longest x16 9.72 us: cholesky_lower(): diagonal_root = jnp.sqrt(partial_col[pivot])]
    ppermute x16 -> x0, waiting for transfers between devices: 22.3 us -> none  [the longest x8 16.3 us: padded_2(): after = lax.ppermute(leading, axis, down)]
    another operation x5 -> x0, other arithmetic: 20.6 us -> none  [the longest x1 19.5 us: upper_solve_transposed(): return jnp.stack(solved, axis=0)]
  transfers between devices with their start and end apart: 16 -> 0, of which waited for: 13 -> 0; matrix products, arithmetic and copies ran while one was open for 1% -> 0% of each run, Pallas kernels for 0% -> 0%
where the time goes in v1:
time: 43.2 us; the launch traced here: 42.9 us
  Pallas kernels  37.2 us (86%)
  local copies, waits for them, and re-layouts  4.38 us (10%)
  between operations  1.33 us (3%)
    pallas_call x1, Pallas kernels, on_device(): pl.pallas_call(functools.partial(kernel, dims), out_shape=(jax.ShapeDtype...  37.2 us
    unnamed x14, local copies, waits for them, and re-layouts  4.38 us

profile of v1, /device:TPU:0, one launch (start us, length us, event | category | flops | bytes accessed | tf_op | source)
XLA Modules:
  0.0 42.9 jit_solution(5646787600876592751)
XLA Ops:
  0.6 0.0 copy-start.2
  1.3 0.0 copy-start.3
  1.3 0.0 copy-start.4
  1.3 0.0 copy-done.2
  1.3 0.6 %copy-done.3 = s32[1,1,128]{2,1,0:T(1,128)S(1)} copy-done((s32[1,1,128]{2,1,0:T(1,128)S(1)}, s32[1,1,128]{2,1,0:T(1,128)}, u32[]{:S(2)}) %copy-start.3) | copy-done | bytes 536
  2.0 0.0 copy-done.4
  2.0 0.0 copy-start
  2.0 1.0 %copy-done = f32[17,6,8,128]{3,2,1,0:T(8,128)S(1)} copy-done((f32[17,6,8,128]{3,2,1,0:T(8,128)S(1)}, f32[17,6,8,128]{3,2,1,0:T(8,128)}, u32[]{:S(2)}) %copy-start) | copy-done | bytes 417816
  3.0 0.0 copy-start.1
  3.0 0.7 %copy-done.1 = f32[17,16]{1,0:T(8,128)S(1)} copy-done((f32[17,16]{1,0:T(8,128)S(1)}, f32[17,16]{1,0:T(8,128)}, u32[]{:S(2)}) %copy-start.1) | copy-done | bytes 1112
  3.7 0.0 copy-start.5
  3.7 0.7 %copy-done.5 = f32[1,1,128]{2,1,0:T(1,128)S(1)} copy-done((f32[1,1,128]{2,1,0:T(1,128)S(1)}, f32[1,1,128]{2,1,0:T(1,128)}, u32[]{:S(2)}) %copy-start.5) | copy-done | bytes 536
  4.3 37.2 %shard_map.86 = (f32[816,128]{1,0:T(8,128)S(1)}, f32[17,17]{1,0:T(8,128)S(1)}) custom-call(f32[816,128]{1,0:T(8,128)S(1)} %bitcast.5, s32[1,128]{1,0:T(1,128)S(1)} %bitcast.7, s32[1,1]{1,0:T(1,128)S(6)} %copy.11.count_ref, f32[1,128]{1,0:T(1,128)S(1)} %bitcast.8, f32[1,128]{1,0:T(1,128)S(1)} %bitcast.9, f32[16,128]{1,0:T(8,128)S(1)} %copy-done.2, ...), custom_call_target="tpu_custom_call" | custom-call | tf_op jit(solution)/shard_map/pallas_call | solution.py:322
  41.6 0.8 %copy.12 = f32[17,6,8,128]{3,2,1,0:T(8,128)} copy(f32[17,6,8,128]{3,2,1,0:T(8,128)S(1)} %bitcast.6) | data formatting | bytes 835584
  42.3 0.6 %copy.13 = f32[17,17]{1,0:T(8,128)} copy(f32[17,17]{1,0:T(8,128)S(1)} %get-tuple-element.9) | data formatting | bytes 2312
Async XLA Ops:
  0.6 0.7 %copy-start.2 = (f32[16,128]{1,0:T(8,128)S(1)}, f32[16,128]{1,0:T(8,128)}, u32[]{:S(2)}) copy-start(f32[16,128]{1,0:T(8,128)} %constant.4.clone.system_ref) | copy-start | bytes 24580
  1.3 0.7 %copy-start.3 = (s32[1,1,128]{2,1,0:T(1,128)S(1)}, s32[1,1,128]{2,1,0:T(1,128)}, u32[]{:S(2)}) copy-start(s32[1,1,128]{2,1,0:T(1,128)} %param.8) | copy-start | bytes 1540
  1.3 0.7 %copy-start.4 = (f32[1,1,128]{2,1,0:T(1,128)S(1)}, f32[1,1,128]{2,1,0:T(1,128)}, u32[]{:S(2)}) copy-start(f32[1,1,128]{2,1,0:T(1,128)} %param.10) | copy-start | bytes 1540
  2.0 1.0 %copy-start = (f32[17,6,8,128]{3,2,1,0:T(8,128)S(1)}, f32[17,6,8,128]{3,2,1,0:T(8,128)}, u32[]{:S(2)}) copy-start(f32[17,6,8,128]{3,2,1,0:T(8,128)} %param.7) | copy-start | bytes 1253380
  3.0 0.7 %copy-start.1 = (f32[17,16]{1,0:T(8,128)S(1)}, f32[17,16]{1,0:T(8,128)}, u32[]{:S(2)}) copy-start(f32[17,16]{1,0:T(8,128)} %constant.5.clone.omega_ref) | copy-start | bytes 3268
  3.7 0.7 %copy-start.5 = (f32[1,1,128]{2,1,0:T(1,128)S(1)}, f32[1,1,128]{2,1,0:T(1,128)}, u32[]{:S(2)}) copy-start(f32[1,1,128]{2,1,0:T(1,128)} %param.11) | copy-start | bytes 1540

commit v2 on v1

--- a/solution.py
+++ b/solution.py
@@ -3,7 +3,6 @@
 
 import jax
 import jax.numpy as jnp
-import numpy as np
 from jax import lax
 from jax.experimental import pallas as pl
 from jax.experimental.pallas import tpu as pltpu
@@ -21,6 +20,7 @@
 MESH = pl.DeviceIdType.MESH
 
 SYS = 32
+BATCH = 4
 
 
 def split2(x):
@@ -48,11 +48,13 @@
 
 
 def kernel(
-    dims, x_ref, index_ref, count_ref, value_ref, weight_ref, system_ref, omega_ref,
+    dims, x_hbm, index_hbm, count_hbm, value_hbm, weight_hbm,
     out_ref, spread_ref,
-    state, send_low, send_high, send_cols, from_north, from_south, from_east, from_west,
-    surface, selector, means, modes, parts, gather_lon, gather_lat,
-    halo_send, halo_recv, lon_send, lon_recv, lat_send, lat_recv,
+    index_ref, count_ref, value_ref, weight_ref, state, send_low, send_high, send_cols, from_north, from_south, from_east, from_west,
+    surface, selector, means, modes, parts,
+    obs_lon, obs_lat, gram_lon, gram_lat, load_sem, halo_send, halo_recv,
+    obs_lon_send, obs_lon_recv, obs_lat_send, obs_lat_recv,
+    gram_lon_send, gram_lon_recv, gram_lat_send, gram_lat_recv,
 ):
     members, fields, rows, cols, n_lat, n_lon = dims
     dirs = members - 1
@@ -72,6 +74,28 @@
     for partner in partners:
         pl.semaphore_signal(barrier, inc=1, device_id=partner, device_id_type=MESH)
 
+    loads = [
+        pltpu.make_async_copy(source, target, load_sem.at[number])
+        for number, (source, target) in enumerate((
+            (x_hbm, state.at[0]),
+            (index_hbm, index_ref),
+            (count_hbm, count_ref),
+            (value_hbm, value_ref),
+            (weight_hbm, weight_ref),
+        ))
+    ]
+    for load in loads:
+        load.start()
+
+    @pl.when(me_lat == n_lat - 1)
+    def _():
+        from_north[...] = jnp.zeros_like(from_north)
+
+    @pl.when(me_lat == 0)
+    def _():
+        from_south[...] = jnp.zeros_like(from_south)
+
+    surface[...] = jnp.zeros_like(surface)
     lane = lax.broadcasted_iota(jnp.int32, (rows, cols), 1)
     row = lax.broadcasted_iota(jnp.int32, (rows, cols), 0)
     half = lane // 2
@@ -96,26 +120,18 @@
         send_cols[slot, 0:rows, :] = packed[0]
         send_cols[slot, rows : 2 * rows, :] = packed[1]
 
+    for load in loads:
+        load.wait()
     packed = [jnp.zeros((rows, cols), jnp.float32)] * 2
     for tile in range(tiles):
-        quantity = x_ref[tile * rows : (tile + 1) * rows, :]
-        state[0, tile * rows : (tile + 1) * rows, :] = quantity
+        quantity = state[0, tile * rows : (tile + 1) * rows, :]
         put_edges(0, tile, quantity)
         pack(packed, tile, quantity)
     put_cols(0, packed)
 
-    for r in range(rows):
-        cell = lax.broadcasted_iota(jnp.int32, (cols, slots), 0) + r * cols
-        hit = jnp.where(cell == index_ref[...], 1.0, 0.0)
-        selector[r * cols : (r + 1) * cols, :] = hit.astype(jnp.bfloat16)
-    live = lax.broadcasted_iota(jnp.int32, (1, slots), 1) < count_ref[...]
-    weight = jnp.where(live, weight_ref[...], 0.0) / (slots * n_lat * n_lon)
-    surface[...] = jnp.zeros_like(surface)
-
     pl.semaphore_wait(barrier, len(partners))
 
-    def substep(step, carry):
-        now, later = lax.rem(step, 2), lax.rem(step + 1, 2)
+    def exchange(step):
         copies = []
         for number, (source, target, device) in enumerate((
             (send_low, from_north, lat_at(-1)),
@@ -123,20 +139,57 @@
             (send_cols, from_east, lon_at(-1)),
             (send_cols, from_west, lon_at(1)),
         )):
-            copy = pltpu.make_async_remote_copy(
+            copies.append(pltpu.make_async_remote_copy(
                 src_ref=source.at[step],
                 dst_ref=target.at[step],
                 send_sem=halo_send.at[step, number],
                 recv_sem=halo_recv.at[step, number],
                 device_id=device,
                 device_id_type=MESH,
-            )
-            copy.start()
-            copies.append(copy)
-        for copy in copies:
-            copy.wait()
-        north_on = jnp.where(me_lat < n_lat - 1, 1.0, 0.0)
-        south_on = jnp.where(me_lat > 0, 1.0, 0.0)
+            ))
+        return copies
+
+    def exchange_start(step):
+        to_south, to_north, to_west, to_east = exchange(step)
+
+        @pl.when(me_lat > 0)
+        def _():
+            to_south.start()
+
+        @pl.when(me_lat < n_lat - 1)
+        def _():
+            to_north.start()
+
+        to_west.start()
+        to_east.start()
+
+    def exchange_end(step):
+        to_south, to_north, to_west, to_east = exchange(step)
+
+        @pl.when(me_lat > 0)
+        def _():
+            to_south.wait_send()
+            to_north.wait_recv()
+
+        @pl.when(me_lat < n_lat - 1)
+        def _():
+            to_north.wait_send()
+            to_south.wait_recv()
+
+        to_west.wait()
+        to_east.wait()
+
+    exchange_start(0)
+    for r in range(rows):
+        cell = lax.broadcasted_iota(jnp.int32, (cols, slots), 0) + r * cols
+        hit = jnp.where(cell == index_ref[...], 1.0, 0.0)
+        selector[r * cols : (r + 1) * cols, :] = hit.astype(jnp.bfloat16)
+    live = lax.broadcasted_iota(jnp.int32, (1, slots), 1) < count_ref[...]
+    weight = jnp.where(live, weight_ref[...], 0.0) / (slots * n_lat * n_lon)
+
+    def substep(step, carry):
+        now, later = lax.rem(step, 2), lax.rem(step + 1, 2)
+        exchange_end(step)
         columns = []
         for parity in range(2):
             east = pltpu.roll(from_east[step, parity * rows : (parity + 1) * rows, :], cols - 1, 1)
@@ -151,8 +204,8 @@
                 base = tile - tile % 2
                 q = state[now, tile * rows : (tile + 1) * rows, :]
                 side = pltpu.roll(columns[tile % 2], cols - 1 - base, 1)
-                above = from_north[step, tile : tile + 1, :] * north_on
-                below = from_south[step, tile : tile + 1, :] * south_on
+                above = from_north[step, tile : tile + 1, :]
+                below = from_south[step, tile : tile + 1, :]
                 here.append(q)
                 east.append(jnp.where(last_lane, side, pltpu.roll(q, cols - 1, 1)))
                 west.append(jnp.where(first_lane, side, pltpu.roll(q, 1, 1)))
@@ -188,10 +241,49 @@
                 pack(packed, tile, after[field])
             surface[member * rows : (member + 1) * rows, :] = after[0] + after[3]
         put_cols(step + 1, packed)
+
+        @pl.when(step + 1 < SUBSTEPS)
+        def _():
+            exchange_start(step + 1)
+
         return carry
 
     lax.fori_loop(0, SUBSTEPS, substep, 0)
     final = SUBSTEPS % 2
+
+    def gather(buffer, me, count, device_of, send, recv):
+        copies = []
+        for d in range(1, count):
+            copy = pltpu.make_async_remote_copy(
+                src_ref=buffer.at[me],
+                dst_ref=buffer.at[me],
+                send_sem=send.at[d],
+                recv_sem=recv.at[me],
+                device_id=device_of(d),
+                device_id_type=MESH,
+            )
+            copy.start()
+            copies.append(copy)
+
+        def total():
+            for d in range(1, count):
+                other = lax.rem(me + d, count)
+                pltpu.make_async_remote_copy(
+                    src_ref=buffer.at[other],
+                    dst_ref=buffer.at[other],
+                    send_sem=send.at[d],
+                    recv_sem=recv.at[other],
+                    device_id=device_of(d),
+                    device_id_type=MESH,
+                ).wait_recv()
+            for copy in copies:
+                copy.wait_send()
+            result = buffer[0]
+            for i in range(1, count):
+                result = result + buffer[i]
+            return result
+
+        return total
 
     pad = surface.shape[0] // rows
     observed = jnp.zeros((3 * pad, slots), jnp.float32)
@@ -208,8 +300,9 @@
     right = jnp.concatenate(
         [jnp.zeros((SYS, slots), jnp.float32), anomaly, jnp.where(top, innovation, 0.0)], axis=0
     )
-    gather_lon[me_lon] = jnp.zeros(gather_lon.shape[1:], jnp.float32)
-    gather_lon[me_lon, 0:dirs, 0 : right.shape[0]] = dot_nt(anomaly * weight, right, highest)
+    obs_lon[me_lon] = jnp.zeros(obs_lon.shape[1:], jnp.float32)
+    obs_lon[me_lon, :, 0 : right.shape[0]] = dot_nt(anomaly * weight, right, highest)
+    obs_on_lon = gather(obs_lon, me_lon, n_lon, lon_at, obs_lon_send, obs_lon_recv)
 
     for field in range(fields):
         total = state[final, field * rows : (field + 1) * rows, :]
@@ -226,67 +319,46 @@
         parts[0:dirs, line * cols : (line + 1) * cols] = high
         parts[dirs : 2 * dirs, line * cols : (line + 1) * cols] = low
     high, low = parts[0:dirs, :], parts[dirs : 2 * dirs, :]
-    gather_lon[me_lon, dirs : 2 * dirs, 0:dirs] = (
-        dot_nt(high, high) + dot_nt(high, low) + dot_nt(low, high)
-    )
-
-    def gather(buffer, me, count, device_of, send, recv):
-        copies = []
-        for d in range(1, count):
-            copy = pltpu.make_async_remote_copy(
-                src_ref=buffer.at[me],
-                dst_ref=buffer.at[me],
-                send_sem=send.at[d],
-                recv_sem=recv.at[me],
-                device_id=device_of(d),
-                device_id_type=MESH,
-            )
-            copy.start()
-            copies.append(copy)
-        for d in range(1, count):
-            other = lax.rem(me + d, count)
-            pltpu.make_async_remote_copy(
-                src_ref=buffer.at[other],
-                dst_ref=buffer.at[other],
-                send_sem=send.at[d],
-                recv_sem=recv.at[other],
-                device_id=device_of(d),
-                device_id_type=MESH,
-            ).wait_recv()
-        for copy in copies:
-            copy.wait_send()
-        total = buffer[0]
-        for i in range(1, count):
-            total = total + buffer[i]
-        return total
-
-    gather_lat[me_lat] = gather(gather_lon, me_lon, n_lon, lon_at, lon_send, lon_recv)
-    total = gather(gather_lat, me_lat, n_lat, lat_at, lat_send, lat_recv)
-
-    system = total[0:dirs] + system_ref[...]
-    mode_gram = total[dirs : 2 * dirs, 0:dirs]
-    below = lax.broadcasted_iota(jnp.int32, system.shape, 0)
-    across = lax.broadcasted_iota(jnp.int32, system.shape, 1)
-    for j in range(dirs):
-        pivot = system[j : j + 1, SYS + j : SYS + j + 1]
-        column = system[:, SYS + j : SYS + j + 1]
-        factor = jnp.where(below > j, column / pivot, 0.0)
-        system = system - factor * system[j : j + 1, :]
+    gram_lon[me_lon] = jnp.zeros(gram_lon.shape[1:], jnp.float32)
+    gram_lon[me_lon, :, 0:dirs] = dot_nt(high, high) + dot_nt(high, low) + dot_nt(low, high)
+    gram_on_lon = gather(gram_lon, me_lon, n_lon, lon_at, gram_lon_send, gram_lon_recv)
+
+    obs_lat[me_lat] = obs_on_lon()
+    obs_on_lat = gather(obs_lat, me_lat, n_lat, lat_at, obs_lat_send, obs_lat_recv)
+    gram_lat[me_lat] = gram_on_lon()
+    gram_on_lat = gather(gram_lat, me_lat, n_lat, lat_at, gram_lat_send, gram_lat_recv)
+
+    below = lax.broadcasted_iota(jnp.int32, (dirs, 128), 0)
+    across = lax.broadcasted_iota(jnp.int32, (dirs, 128), 1)
+    identity = jnp.where(across == below, 1.0, 0.0)
+    inside = (across >= SYS) & (across < SYS + dirs)
+    gamma = jnp.where(across == below + SYS, 1.0, 0.0) - jnp.where(inside, 1.0 / members, 0.0)
+    system = obs_on_lat() + (identity + dirs / forget * gamma)
+    for start in range(0, dirs, BATCH):
+        batch = [
+            jnp.broadcast_to(system[:, SYS + j : SYS + j + 1], system.shape)
+            for j in range(start, start + BATCH)
+        ]
+        for i in range(BATCH):
+            j = start + i
+            factor = jnp.where(below > j, batch[i] * (1.0 / batch[i][j : j + 1, :]), 0.0)
+            for k in range(i + 1, BATCH):
+                batch[k] = batch[k] - factor * batch[k][j : j + 1, :]
+            system = system - factor * system[j : j + 1, :]
     diagonal = jnp.sum(jnp.where(across == below + SYS, system, 0.0), axis=1, keepdims=True)
     system = system / jnp.sqrt(diagonal)
     solved = system[:, SYS + dirs : SYS + dirs + 1]
     inverse = system[:, 0:dirs]
     weights = jnp.sum(solved * inverse, axis=0, keepdims=True)
+    shift = (math.sqrt(members) - 1.0) / dirs
+    body = (shift - 1.0) / members
+    tail = -math.sqrt(members) / members
+    place = lax.broadcasted_iota(jnp.int32, (members, dirs), 0)
+    mode = lax.broadcasted_iota(jnp.int32, (members, dirs), 1)
+    omega = jnp.where(place == dirs, tail, jnp.where(place == mode, 1.0 + body, body))
     rotation = jnp.dot(
-        omega_ref[...], inverse, precision=highest, preferred_element_type=jnp.float32
-    )
-    spread = dot_nt(
-        jnp.dot(rotation, mode_gram, precision=highest, preferred_element_type=jnp.float32),
-        rotation,
-        highest,
-    )
-    spread_ref[...] = spread * (1.0 / (fields * cells * n_lat * n_lon))
-
+        math.sqrt(dirs) * omega, inverse, precision=highest, preferred_element_type=jnp.float32
+    )
     c_high, c_low = split2(rotation + weights)
     for field in range(fields):
         block = pl.ds(field * cells, cells)
@@ -298,16 +370,13 @@
                 update[:, r * cols : (r + 1) * cols] + means[line : line + 1, :]
             )
 
-
-def constants(members):
-    dirs = members - 1
-    identity = np.eye(dirs)
-    system = np.zeros((dirs, 128))
-    system[:, 0:dirs] = identity
-    system[:, SYS : SYS + dirs] = dirs / forget * (identity - 1.0 / members)
-    projector = np.concatenate([identity, np.zeros((1, dirs))], axis=0) - 1.0 / members
-    omega = projector @ (identity + (math.sqrt(members) - 1.0) / dirs)
-    return system.astype(np.float32), (math.sqrt(dirs) * omega).astype(np.float32)
+    mode_gram = gram_on_lat()[:, 0:dirs]
+    spread = dot_nt(
+        jnp.dot(rotation, mode_gram, precision=highest, preferred_element_type=jnp.float32),
+        rotation,
+        highest,
+    )
+    spread_ref[...] = spread * (1.0 / (fields * cells * n_lat * n_lon))
 
 
 def on_device(n_lat, n_lon, sample_collection, obs_index, obs_count, obs_value, obs_weight):
@@ -316,7 +385,6 @@
     dirs, tiles = members - 1, members * fields
     padded_tiles = -(-tiles // 8) * 8
     pad = -(-members // 16) * 16
-    system, omega = constants(members)
     f32 = jnp.float32
     dims = (members, fields, rows, cols, n_lat, n_lon)
     analysis, spread = pl.pallas_call(
@@ -325,9 +393,13 @@
             jax.ShapeDtypeStruct((tiles * rows, cols), f32),
             jax.ShapeDtypeStruct((members, members), f32),
         ),
-        in_specs=[pl.BlockSpec(memory_space=pltpu.VMEM)] * 7,
+        in_specs=[pl.BlockSpec(memory_space=pl.ANY)] * 5,
         out_specs=(pl.BlockSpec(memory_space=pltpu.VMEM),) * 2,
         scratch_shapes=[
+            pltpu.VMEM((1, slots), jnp.int32),
+            pltpu.VMEM((1, 1), jnp.int32),
+            pltpu.VMEM((1, slots), f32),
+            pltpu.VMEM((1, slots), f32),
             pltpu.VMEM((2, tiles * rows, cols), f32),
             pltpu.VMEM((SUBSTEPS + 1, padded_tiles, cols), f32),
             pltpu.VMEM((SUBSTEPS + 1, padded_tiles, cols), f32),
@@ -341,15 +413,15 @@
             pltpu.VMEM((fields * rows, cols), f32),
             pltpu.VMEM((dirs * fields * rows, cols), f32),
             pltpu.VMEM((2 * dirs, fields * rows * cols), jnp.bfloat16),
-            pltpu.VMEM((n_lon, 2 * dirs, 128), f32),
-            pltpu.VMEM((n_lat, 2 * dirs, 128), f32),
+            pltpu.VMEM((n_lon, dirs, 128), f32),
+            pltpu.VMEM((n_lat, dirs, 128), f32),
+            pltpu.VMEM((n_lon, dirs, 128), f32),
+            pltpu.VMEM((n_lat, dirs, 128), f32),
+            pltpu.SemaphoreType.DMA((5,)),
             pltpu.SemaphoreType.DMA((SUBSTEPS, 4)),
             pltpu.SemaphoreType.DMA((SUBSTEPS, 4)),
-            pltpu.SemaphoreType.DMA((n_lon,)),
-            pltpu.SemaphoreType.DMA((n_lon,)),
-            pltpu.SemaphoreType.DMA((n_lat,)),
-            pltpu.SemaphoreType.DMA((n_lat,)),
-        ],
+        ]
+        + [pltpu.SemaphoreType.DMA((n,)) for n in (n_lon, n_lon, n_lat, n_lat) * 2],
         compiler_params=pltpu.CompilerParams(
             collective_id=0, has_side_effects=True, vmem_limit_bytes=32 * 1024 * 1024
         ),
@@ -359,8 +431,6 @@
         obs_count.reshape(1, 1),
         obs_value.reshape(1, slots),
         obs_weight.reshape(1, slots),
-        jnp.asarray(system),
-        jnp.asarray(omega),
     )
     return analysis.reshape(sample_collection.shape), spread
 

time: 43.2 us -> 40.1 us (0.928)
  Pallas kernels: 37.2 us -> 35.6 us
  local copies, waits for them, and re-layouts: 4.38 us -> 3.02 us
    pallas_call x1, Pallas kernels: 37.2 us -> 35.6 us  [on_device(): pl.pallas_call(functools.partial(kernel, dims), out_shape=(jax.ShapeDtype...]
    unnamed x14 -> x10, local copies, waits for them, and re-layouts: 4.38 us -> 3.02 us
where the time goes in v2:
time: 40.1 us; the launch traced here: 39.9 us
  Pallas kernels  35.6 us (89%)
  local copies, waits for them, and re-layouts  3.02 us (8%)
  between operations  1.31 us (3%)
    pallas_call x1, Pallas kernels, on_device(): pl.pallas_call(functools.partial(kernel, dims), out_shape=(jax.ShapeDtype...  35.6 us
    unnamed x10, local copies, waits for them, and re-layouts  3.02 us

profile of v2, /device:TPU:0, one launch (start us, length us, event | category | flops | bytes accessed | tf_op | source)
XLA Modules:
  0.0 39.9 jit_solution(1555792610450176727)
XLA Ops:
  1.3 0.0 copy-start.1
  1.3 0.0 copy-start.2
  1.3 0.0 copy-start.3
  1.3 0.6 %copy-done.1 = s32[1,1,128]{2,1,0:T(1,128)S(1)} copy-done((s32[1,1,128]{2,1,0:T(1,128)S(1)}, s32[1,1,128]{2,1,0:T(1,128)}, u32[]{:S(2)}) %copy-start.1) | copy-done | bytes 536
  1.9 0.0 copy-done.2
  1.9 0.0 copy-done.3
  2.0 0.0 copy-start
  2.0 1.0 %copy-done = f32[17,6,8,128]{3,2,1,0:T(8,128)S(1)} copy-done((f32[17,6,8,128]{3,2,1,0:T(8,128)S(1)}, f32[17,6,8,128]{3,2,1,0:T(8,128)}, u32[]{:S(2)}) %copy-start) | copy-done | bytes 417816
  3.0 35.6 %shard_map.68 = (f32[816,128]{1,0:T(8,128)S(1)}, f32[17,17]{1,0:T(8,128)S(1)}) custom-call(f32[816,128]{1,0:T(8,128)S(1)} %bitcast.5, s32[1,128]{1,0:T(1,128)S(1)} %bitcast.7, s32[1,1]{1,0:T(1,128)S(6)} %copy.9.count_hbm, f32[1,128]{1,0:T(1,128)S(1)} %bitcast.8, f32[1,128]{1,0:T(1,128)S(1)} %bitcast.9), custom_call_target="tpu_custom_call" | custom-call | tf_op jit(solution)/shard_map/pallas_call | solution.py:390
  38.5 0.8 %copy.10 = f32[17,6,8,128]{3,2,1,0:T(8,128)} copy(f32[17,6,8,128]{3,2,1,0:T(8,128)S(1)} %bitcast.6) | data formatting | bytes 835584
  39.3 0.6 %copy.11 = f32[17,17]{1,0:T(8,128)} copy(f32[17,17]{1,0:T(8,128)S(1)} %get-tuple-element.9) | data formatting | bytes 2312
Async XLA Ops:
  1.3 0.7 %copy-start.1 = (s32[1,1,128]{2,1,0:T(1,128)S(1)}, s32[1,1,128]{2,1,0:T(1,128)}, u32[]{:S(2)}) copy-start(s32[1,1,128]{2,1,0:T(1,128)} %param.6) | copy-start | bytes 1540
  1.3 0.7 %copy-start.2 = (f32[1,1,128]{2,1,0:T(1,128)S(1)}, f32[1,1,128]{2,1,0:T(1,128)}, u32[]{:S(2)}) copy-start(f32[1,1,128]{2,1,0:T(1,128)} %param.8) | copy-start | bytes 1540
  1.3 0.7 %copy-start.3 = (f32[1,1,128]{2,1,0:T(1,128)S(1)}, f32[1,1,128]{2,1,0:T(1,128)}, u32[]{:S(2)}) copy-start(f32[1,1,128]{2,1,0:T(1,128)} %param.9) | copy-start | bytes 1540
  2.0 1.0 %copy-start = (f32[17,6,8,128]{3,2,1,0:T(8,128)S(1)}, f32[17,6,8,128]{3,2,1,0:T(8,128)}, u32[]{:S(2)}) copy-start(f32[17,6,8,128]{3,2,1,0:T(8,128)} %param.5) | copy-start | bytes 1253380

commit v3 on v2

--- a/solution.py
+++ b/solution.py
@@ -50,7 +50,8 @@
 def kernel(
     dims, x_hbm, index_hbm, count_hbm, value_hbm, weight_hbm,
     out_ref, spread_ref,
-    index_ref, count_ref, value_ref, weight_ref, state, send_low, send_high, send_cols, from_north, from_south, from_east, from_west,
+    index_ref, count_ref, value_ref, weight_ref,
+    state, send_low, send_high, send_cols, from_north, from_south, from_east, from_west,
     surface, selector, means, modes, parts,
     obs_lon, obs_lat, gram_lon, gram_lat, load_sem, halo_send, halo_recv,
     obs_lon_send, obs_lon_recv, obs_lat_send, obs_lat_recv,
@@ -102,84 +103,78 @@
     first_lane, last_lane = lane == 0, lane == cols - 1
     first_row, last_row = row == 0, row == rows - 1
     even_lane = (lane - 2 * half) == 0
+    edge_lane = first_lane | last_lane
     row_number = (row + me_lat * rows).astype(jnp.float32)
     coriolis = coriolis_scale * (2.0 * (row_number + 0.5) / (rows * n_lat) - 1.0)
     turn = time_step * coriolis
     ghost = 0.5 * time_step
 
-    def pack(packed, tile, quantity):
-        base = tile - tile % 2
-        moved = pltpu.roll(quantity, base + 1, 1)
-        packed[tile % 2] = jnp.where(half == base // 2, moved, packed[tile % 2])
-
-    def put_edges(slot, tile, quantity):
-        send_low[slot, tile : tile + 1, :] = quantity[0:1, :]
-        send_high[slot, tile : tile + 1, :] = quantity[rows - 1 : rows, :]
-
-    def put_cols(slot, packed):
-        send_cols[slot, 0:rows, :] = packed[0]
-        send_cols[slot, rows : 2 * rows, :] = packed[1]
-
-    for load in loads:
-        load.wait()
-    packed = [jnp.zeros((rows, cols), jnp.float32)] * 2
-    for tile in range(tiles):
-        quantity = state[0, tile * rows : (tile + 1) * rows, :]
-        put_edges(0, tile, quantity)
-        pack(packed, tile, quantity)
-    put_cols(0, packed)
-
-    pl.semaphore_wait(barrier, len(partners))
-
-    def exchange(step):
-        copies = []
-        for number, (source, target, device) in enumerate((
+    def put_edges(slot, now):
+        for field in range(fields):
+            packed = jnp.zeros((rows, cols), jnp.float32)
+            for member in range(members):
+                at = (member * fields + field) * rows
+                moved = pltpu.roll(state[now, at : at + rows, :], 2 * member + 1, 1)
+                packed = jnp.where(half == member, moved, packed)
+            send_cols[slot, field * rows : (field + 1) * rows, :] = packed
+        exchange_start(slot, "lon")
+        for tile in range(tiles):
+            send_low[slot, tile : tile + 1, :] = state[now, tile * rows : tile * rows + 1, :]
+            last = (tile + 1) * rows - 1
+            send_high[slot, tile : tile + 1, :] = state[now, last : last + 1, :]
+        exchange_start(slot, "lat")
+
+    def halo_copy(step, number):
+        source, target, device = (
             (send_low, from_north, lat_at(-1)),
             (send_high, from_south, lat_at(1)),
             (send_cols, from_east, lon_at(-1)),
             (send_cols, from_west, lon_at(1)),
-        )):
-            copies.append(pltpu.make_async_remote_copy(
-                src_ref=source.at[step],
-                dst_ref=target.at[step],
-                send_sem=halo_send.at[step, number],
-                recv_sem=halo_recv.at[step, number],
-                device_id=device,
-                device_id_type=MESH,
-            ))
-        return copies
-
-    def exchange_start(step):
-        to_south, to_north, to_west, to_east = exchange(step)
+        )[number]
+        return pltpu.make_async_remote_copy(
+            src_ref=source.at[step],
+            dst_ref=target.at[step],
+            send_sem=halo_send.at[step, number],
+            recv_sem=halo_recv.at[step, number],
+            device_id=device,
+            device_id_type=MESH,
+        )
+
+    def exchange_start(step, axis):
+        if axis == "lon":
+            halo_copy(step, 2).start()
+            halo_copy(step, 3).start()
+            return
 
         @pl.when(me_lat > 0)
         def _():
-            to_south.start()
+            halo_copy(step, 0).start()
 
         @pl.when(me_lat < n_lat - 1)
         def _():
-            to_north.start()
-
-        to_west.start()
-        to_east.start()
-
-    def exchange_end(step):
-        to_south, to_north, to_west, to_east = exchange(step)
+            halo_copy(step, 1).start()
+
+    def exchange_end(step, axis):
+        if axis == "lon":
+            halo_copy(step, 2).wait()
+            halo_copy(step, 3).wait()
+            return
 
         @pl.when(me_lat > 0)
         def _():
-            to_south.wait_send()
-            to_north.wait_recv()
+            halo_copy(step, 0).wait_send()
+            halo_copy(step, 1).wait_recv()
 
         @pl.when(me_lat < n_lat - 1)
         def _():
-            to_north.wait_send()
-            to_south.wait_recv()
-
-        to_west.wait()
-        to_east.wait()
-
-    exchange_start(0)
+            halo_copy(step, 1).wait_send()
+            halo_copy(step, 0).wait_recv()
+
+    for load in loads:
+        load.wait()
+    pl.semaphore_wait(barrier, len(partners))
+    put_edges(0, 0)
+
     for r in range(rows):
         cell = lax.broadcasted_iota(jnp.int32, (cols, slots), 0) + r * cols
         hit = jnp.where(cell == index_ref[...], 1.0, 0.0)
@@ -187,30 +182,30 @@
     live = lax.broadcasted_iota(jnp.int32, (1, slots), 1) < count_ref[...]
     weight = jnp.where(live, weight_ref[...], 0.0) / (slots * n_lat * n_lon)
 
+    def halo_terms(halo, edge, across, side):
+        pressure = halo[0] + halo[3]
+        terms = []
+        for layer, depth in enumerate((depth_top, depth_low)):
+            h, u, v = halo[3 * layer : 3 * layer + 3]
+            speed = edge[3 * layer + across]
+            slope = [(depth + h) * (u, v)[across - 1], speed * u, speed * v]
+            slope[across] = slope[across] + pressure
+            terms += [0.25 * q - side * d for q, d in zip((h, u, v), slope)]
+            pressure = pressure + grav_low * halo[3]
+        return terms
+
     def substep(step, carry):
         now, later = lax.rem(step, 2), lax.rem(step + 1, 2)
-        exchange_end(step)
-        columns = []
-        for parity in range(2):
-            east = pltpu.roll(from_east[step, parity * rows : (parity + 1) * rows, :], cols - 1, 1)
-            west = pltpu.roll(from_west[step, parity * rows : (parity + 1) * rows, :], 1, 1)
-            columns.append(jnp.where(even_lane, east, west))
-
-        packed = [jnp.zeros((rows, cols), jnp.float32)] * 2
         for member in range(members):
             here, east, west, north, south = [], [], [], [], []
             for field in range(fields):
                 tile = member * fields + field
-                base = tile - tile % 2
                 q = state[now, tile * rows : (tile + 1) * rows, :]
-                side = pltpu.roll(columns[tile % 2], cols - 1 - base, 1)
-                above = from_north[step, tile : tile + 1, :]
-                below = from_south[step, tile : tile + 1, :]
                 here.append(q)
-                east.append(jnp.where(last_lane, side, pltpu.roll(q, cols - 1, 1)))
-                west.append(jnp.where(first_lane, side, pltpu.roll(q, 1, 1)))
-                north.append(jnp.where(last_row, above, pltpu.roll(q, rows - 1, 0)))
-                south.append(jnp.where(first_row, below, pltpu.roll(q, 1, 0)))
+                east.append(jnp.where(last_lane, 0.0, pltpu.roll(q, cols - 1, 1)))
+                west.append(jnp.where(first_lane, 0.0, pltpu.roll(q, 1, 1)))
+                north.append(jnp.where(last_row, 0.0, pltpu.roll(q, rows - 1, 0)))
+                south.append(jnp.where(first_row, 0.0, pltpu.roll(q, 1, 0)))
             dx = [e - w for e, w in zip(east, west)]
             dy = [n - s for n, s in zip(north, south)]
             mean = [0.25 * ((e + w) + (n + s)) for e, w, n, s in zip(east, west, north, south)]
@@ -237,14 +232,36 @@
             for field in range(fields):
                 tile = member * fields + field
                 state[later, tile * rows : (tile + 1) * rows, :] = after[field]
-                put_edges(step + 1, tile, after[field])
-                pack(packed, tile, after[field])
-            surface[member * rows : (member + 1) * rows, :] = after[0] + after[3]
-        put_cols(step + 1, packed)
+
+        exchange_end(step, "lon")
+        halo, edge = [], []
+        for field in range(fields):
+            block = slice(field * rows, (field + 1) * rows)
+            from_e = pltpu.roll(from_east[step, block, :], cols - 1, 1)
+            from_w = pltpu.roll(from_west[step, block, :], 1, 1)
+            halo.append(jnp.where(even_lane, from_e, from_w))
+            edge.append(send_cols[step, block, :])
+        side = jnp.where(even_lane, ghost, -ghost)
+        for field, added in enumerate(halo_terms(halo, edge, 1, side)):
+            for member in range(members):
+                at = (member * fields + field) * rows
+                moved = pltpu.roll(added, cols - 1 - 2 * member, 1)
+                state[later, at : at + rows, :] += jnp.where(edge_lane, moved, 0.0)
+
+        exchange_end(step, "lat")
+        for source, sent, at_row, side in (
+            (from_north, send_high, rows - 1, ghost),
+            (from_south, send_low, 0, -ghost),
+        ):
+            halo = [source[step, pl.ds(f, members, stride=fields), :] for f in range(fields)]
+            edge = [sent[step, pl.ds(f, members, stride=fields), :] for f in range(fields)]
+            for field, added in enumerate(halo_terms(halo, edge, 2, side)):
+                place = pl.ds(field * rows + at_row, members, stride=fields * rows)
+                state[later, place, :] = state[later, place, :] + added
 
         @pl.when(step + 1 < SUBSTEPS)
         def _():
-            exchange_start(step + 1)
+            put_edges(step + 1, later)
 
         return carry
 
@@ -285,13 +302,16 @@
 
         return total
 
-    pad = surface.shape[0] // rows
+    pad = surface.shape[0]
     observed = jnp.zeros((3 * pad, slots), jnp.float32)
     for r in range(rows):
-        level = surface[pl.ds(r, pad, stride=rows), :]
-        observed += dot(
-            jnp.concatenate(split3(level), axis=0), selector[r * cols : (r + 1) * cols, :]
+        block = slice(r * cols, (r + 1) * cols)
+        surface[0:members, block] = (
+            state[final, pl.ds(r, members, stride=fields * rows), :]
+            + state[final, pl.ds(3 * rows + r, members, stride=fields * rows), :]
         )
+        level = jnp.concatenate(split3(surface[:, block]), axis=0)
+        observed += dot(level, selector[block, :])
     observed = observed[0:pad] + observed[pad : 2 * pad] + observed[2 * pad : 3 * pad]
     obs_mean = jnp.sum(observed, axis=0, keepdims=True) * (1.0 / members)
     anomaly = observed[0:dirs] - obs_mean
@@ -393,7 +413,7 @@
             jax.ShapeDtypeStruct((tiles * rows, cols), f32),
             jax.ShapeDtypeStruct((members, members), f32),
         ),
-        in_specs=[pl.BlockSpec(memory_space=pl.ANY)] * 5,
+        in_specs=[pl.BlockSpec(memory_space=pltpu.HBM)] * 5,
         out_specs=(pl.BlockSpec(memory_space=pltpu.VMEM),) * 2,
         scratch_shapes=[
             pltpu.VMEM((1, slots), jnp.int32),
@@ -401,14 +421,14 @@
             pltpu.VMEM((1, slots), f32),
             pltpu.VMEM((1, slots), f32),
             pltpu.VMEM((2, tiles * rows, cols), f32),
-            pltpu.VMEM((SUBSTEPS + 1, padded_tiles, cols), f32),
-            pltpu.VMEM((SUBSTEPS + 1, padded_tiles, cols), f32),
-            pltpu.VMEM((SUBSTEPS + 1, 2 * rows, cols), f32),
             pltpu.VMEM((SUBSTEPS, padded_tiles, cols), f32),
             pltpu.VMEM((SUBSTEPS, padded_tiles, cols), f32),
-            pltpu.VMEM((SUBSTEPS, 2 * rows, cols), f32),
-            pltpu.VMEM((SUBSTEPS, 2 * rows, cols), f32),
-            pltpu.VMEM((pad * rows, cols), f32),
+            pltpu.VMEM((SUBSTEPS, fields * rows, cols), f32),
+            pltpu.VMEM((SUBSTEPS, padded_tiles, cols), f32),
+            pltpu.VMEM((SUBSTEPS, padded_tiles, cols), f32),
+            pltpu.VMEM((SUBSTEPS, fields * rows, cols), f32),
+            pltpu.VMEM((SUBSTEPS, fields * rows, cols), f32),
+            pltpu.VMEM((pad, rows * cols), f32),
             pltpu.VMEM((rows * cols, slots), jnp.bfloat16),
             pltpu.VMEM((fields * rows, cols), f32),
             pltpu.VMEM((dirs * fields * rows, cols), f32),

time: 40.1 us -> 37.3 us (0.930)
  Pallas kernels: 35.6 us -> 32.8 us
    pallas_call x1, Pallas kernels: 35.6 us -> 32.8 us  [on_device(): pl.pallas_call(functools.partial(kernel, dims), out_shape=(jax.ShapeDtype...]
where the time goes in v3:
time: 37.3 us; the launch traced here: 37.1 us
  Pallas kernels  32.8 us (88%)
  local copies, waits for them, and re-layouts  3.02 us (8%)
  between operations  1.31 us (4%)
    pallas_call x1, Pallas kernels, on_device(): pl.pallas_call(functools.partial(kernel, dims), out_shape=(jax.ShapeDtype...  32.8 us
    unnamed x10, local copies, waits for them, and re-layouts  3.02 us

profile of v3, /device:TPU:0, one launch (start us, length us, event | category | flops | bytes accessed | tf_op | source)
XLA Modules:
  0.0 37.1 jit_solution(10896238861929920442)
XLA Ops:
  1.3 0.0 copy-start.1
  1.3 0.0 copy-start.2
  1.3 0.0 copy-start.3
  1.3 0.6 %copy-done.1 = s32[1,1,128]{2,1,0:T(1,128)S(1)} copy-done((s32[1,1,128]{2,1,0:T(1,128)S(1)}, s32[1,1,128]{2,1,0:T(1,128)}, u32[]{:S(2)}) %copy-start.1) | copy-done | bytes 536
  1.9 0.0 copy-done.2
  1.9 0.0 copy-done.3
  2.0 0.0 copy-start
  2.0 1.0 %copy-done = f32[17,6,8,128]{3,2,1,0:T(8,128)S(1)} copy-done((f32[17,6,8,128]{3,2,1,0:T(8,128)S(1)}, f32[17,6,8,128]{3,2,1,0:T(8,128)}, u32[]{:S(2)}) %copy-start) | copy-done | bytes 417816
  3.0 32.8 %shard_map.68 = (f32[816,128]{1,0:T(8,128)S(1)}, f32[17,17]{1,0:T(8,128)S(1)}) custom-call(f32[816,128]{1,0:T(8,128)S(1)} %bitcast.5, s32[1,128]{1,0:T(1,128)S(1)} %bitcast.7, s32[1,1]{1,0:T(1,128)S(6)} %copy.9.count_hbm, f32[1,128]{1,0:T(1,128)S(1)} %bitcast.8, f32[1,128]{1,0:T(1,128)S(1)} %bitcast.9), custom_call_target="tpu_custom_call" | custom-call | tf_op jit(solution)/shard_map/pallas_call | solution.py:410
  35.7 0.8 %copy.10 = f32[17,6,8,128]{3,2,1,0:T(8,128)} copy(f32[17,6,8,128]{3,2,1,0:T(8,128)S(1)} %bitcast.6) | data formatting | bytes 835584
  36.5 0.6 %copy.11 = f32[17,17]{1,0:T(8,128)} copy(f32[17,17]{1,0:T(8,128)S(1)} %get-tuple-element.9) | data formatting | bytes 2312
Async XLA Ops:
  1.3 0.7 %copy-start.1 = (s32[1,1,128]{2,1,0:T(1,128)S(1)}, s32[1,1,128]{2,1,0:T(1,128)}, u32[]{:S(2)}) copy-start(s32[1,1,128]{2,1,0:T(1,128)} %param.6) | copy-start | bytes 1540
  1.3 0.7 %copy-start.2 = (f32[1,1,128]{2,1,0:T(1,128)S(1)}, f32[1,1,128]{2,1,0:T(1,128)}, u32[]{:S(2)}) copy-start(f32[1,1,128]{2,1,0:T(1,128)} %param.8) | copy-start | bytes 1540
  1.3 0.7 %copy-start.3 = (f32[1,1,128]{2,1,0:T(1,128)S(1)}, f32[1,1,128]{2,1,0:T(1,128)}, u32[]{:S(2)}) copy-start(f32[1,1,128]{2,1,0:T(1,128)} %param.9) | copy-start | bytes 1540
  2.0 1.0 %copy-start = (f32[17,6,8,128]{3,2,1,0:T(8,128)S(1)}, f32[17,6,8,128]{3,2,1,0:T(8,128)}, u32[]{:S(2)}) copy-start(f32[17,6,8,128]{3,2,1,0:T(8,128)} %param.5) | copy-start | bytes 1253380

commit v4 on v3

--- a/solution.py
+++ b/solution.py
@@ -21,6 +21,7 @@
 
 SYS = 32
 BATCH = 4
+GROUPS = 2
 
 
 def split2(x):
@@ -109,22 +110,26 @@
     turn = time_step * coriolis
     ghost = 0.5 * time_step
 
-    def put_edges(slot, now):
+    bounds = [members * g // GROUPS for g in range(GROUPS + 1)]
+
+    def put_edges(slot, group, now):
+        first, last = bounds[group], bounds[group + 1]
         for field in range(fields):
             packed = jnp.zeros((rows, cols), jnp.float32)
-            for member in range(members):
+            for member in range(first, last):
                 at = (member * fields + field) * rows
-                moved = pltpu.roll(state[now, at : at + rows, :], 2 * member + 1, 1)
-                packed = jnp.where(half == member, moved, packed)
-            send_cols[slot, field * rows : (field + 1) * rows, :] = packed
-        exchange_start(slot, "lon")
-        for tile in range(tiles):
-            send_low[slot, tile : tile + 1, :] = state[now, tile * rows : tile * rows + 1, :]
-            last = (tile + 1) * rows - 1
-            send_high[slot, tile : tile + 1, :] = state[now, last : last + 1, :]
-        exchange_start(slot, "lat")
-
-    def halo_copy(step, number):
+                moved = pltpu.roll(state[now, at : at + rows, :], 2 * (member - first) + 1, 1)
+                packed = jnp.where(half == member - first, moved, packed)
+            send_cols[slot, group, field * rows : (field + 1) * rows, :] = packed
+        exchange_start(slot, group, "lon")
+        for tile in range(first * fields, last * fields):
+            place = slice(tile - first * fields, tile - first * fields + 1)
+            low, high = tile * rows, (tile + 1) * rows - 1
+            send_low[slot, group, place, :] = state[now, low : low + 1, :]
+            send_high[slot, group, place, :] = state[now, high : high + 1, :]
+        exchange_start(slot, group, "lat")
+
+    def halo_copy(step, group, number):
         source, target, device = (
             (send_low, from_north, lat_at(-1)),
             (send_high, from_south, lat_at(1)),
@@ -132,48 +137,49 @@
             (send_cols, from_west, lon_at(1)),
         )[number]
         return pltpu.make_async_remote_copy(
-            src_ref=source.at[step],
-            dst_ref=target.at[step],
-            send_sem=halo_send.at[step, number],
-            recv_sem=halo_recv.at[step, number],
+            src_ref=source.at[step, group],
+            dst_ref=target.at[step, group],
+            send_sem=halo_send.at[step, group, number],
+            recv_sem=halo_recv.at[step, group, number],
             device_id=device,
             device_id_type=MESH,
         )
 
-    def exchange_start(step, axis):
+    def exchange_start(step, group, axis):
         if axis == "lon":
-            halo_copy(step, 2).start()
-            halo_copy(step, 3).start()
+            halo_copy(step, group, 2).start()
+            halo_copy(step, group, 3).start()
             return
 
         @pl.when(me_lat > 0)
         def _():
-            halo_copy(step, 0).start()
+            halo_copy(step, group, 0).start()
 
         @pl.when(me_lat < n_lat - 1)
         def _():
-            halo_copy(step, 1).start()
-
-    def exchange_end(step, axis):
+            halo_copy(step, group, 1).start()
+
+    def exchange_end(step, group, axis):
         if axis == "lon":
-            halo_copy(step, 2).wait()
-            halo_copy(step, 3).wait()
+            halo_copy(step, group, 2).wait()
+            halo_copy(step, group, 3).wait()
             return
 
         @pl.when(me_lat > 0)
         def _():
-            halo_copy(step, 0).wait_send()
-            halo_copy(step, 1).wait_recv()
+            halo_copy(step, group, 0).wait_send()
+            halo_copy(step, group, 1).wait_recv()
 
         @pl.when(me_lat < n_lat - 1)
         def _():
-            halo_copy(step, 1).wait_send()
-            halo_copy(step, 0).wait_recv()
+            halo_copy(step, group, 1).wait_send()
+            halo_copy(step, group, 0).wait_recv()
 
     for load in loads:
         load.wait()
     pl.semaphore_wait(barrier, len(partners))
-    put_edges(0, 0)
+    for group in range(GROUPS):
+        put_edges(0, group, 0)
 
     for r in range(rows):
         cell = lax.broadcasted_iota(jnp.int32, (cols, slots), 0) + r * cols
@@ -193,6 +199,40 @@
             terms += [0.25 * q - side * d for q, d in zip((h, u, v), slope)]
             pressure = pressure + grav_low * halo[3]
         return terms
+
+    def finish(step, group, later):
+        first, last = bounds[group], bounds[group + 1]
+        exchange_end(step, group, "lon")
+        halo, edge = [], []
+        for field in range(fields):
+            block = slice(field * rows, (field + 1) * rows)
+            from_e = pltpu.roll(from_east[step, group, block, :], cols - 1, 1)
+            from_w = pltpu.roll(from_west[step, group, block, :], 1, 1)
+            halo.append(jnp.where(even_lane, from_e, from_w))
+            edge.append(send_cols[step, group, block, :])
+        side = jnp.where(even_lane, ghost, -ghost)
+        for field, added in enumerate(halo_terms(halo, edge, 1, side)):
+            for member in range(first, last):
+                at = (member * fields + field) * rows
+                moved = pltpu.roll(added, cols - 1 - 2 * (member - first), 1)
+                state[later, at : at + rows, :] += jnp.where(edge_lane, moved, 0.0)
+
+        exchange_end(step, group, "lat")
+        for source, sent, at_row, side in (
+            (from_north, send_high, rows - 1, ghost),
+            (from_south, send_low, 0, -ghost),
+        ):
+            lines = [pl.ds(field, last - first, stride=fields) for field in range(fields)]
+            halo = [source[step, group, line, :] for line in lines]
+            edge = [sent[step, group, line, :] for line in lines]
+            for field, added in enumerate(halo_terms(halo, edge, 2, side)):
+                at = (first * fields + field) * rows + at_row
+                place = pl.ds(at, last - first, stride=fields * rows)
+                state[later, place, :] = state[later, place, :] + added
+
+        @pl.when(step + 1 < SUBSTEPS)
+        def _():
+            put_edges(step + 1, group, later)
 
     def substep(step, carry):
         now, later = lax.rem(step, 2), lax.rem(step + 1, 2)
@@ -233,36 +273,8 @@
                 tile = member * fields + field
                 state[later, tile * rows : (tile + 1) * rows, :] = after[field]
 
-        exchange_end(step, "lon")
-        halo, edge = [], []
-        for field in range(fields):
-            block = slice(field * rows, (field + 1) * rows)
-            from_e = pltpu.roll(from_east[step, block, :], cols - 1, 1)
-            from_w = pltpu.roll(from_west[step, block, :], 1, 1)
-            halo.append(jnp.where(even_lane, from_e, from_w))
-            edge.append(send_cols[step, block, :])
-        side = jnp.where(even_lane, ghost, -ghost)
-        for field, added in enumerate(halo_terms(halo, edge, 1, side)):
-            for member in range(members):
-                at = (member * fields + field) * rows
-                moved = pltpu.roll(added, cols - 1 - 2 * member, 1)
-                state[later, at : at + rows, :] += jnp.where(edge_lane, moved, 0.0)
-
-        exchange_end(step, "lat")
-        for source, sent, at_row, side in (
-            (from_north, send_high, rows - 1, ghost),
-            (from_south, send_low, 0, -ghost),
-        ):
-            halo = [source[step, pl.ds(f, members, stride=fields), :] for f in range(fields)]
-            edge = [sent[step, pl.ds(f, members, stride=fields), :] for f in range(fields)]
-            for field, added in enumerate(halo_terms(halo, edge, 2, side)):
-                place = pl.ds(field * rows + at_row, members, stride=fields * rows)
-                state[later, place, :] = state[later, place, :] + added
-
-        @pl.when(step + 1 < SUBSTEPS)
-        def _():
-            put_edges(step + 1, later)
-
+        for group in range(GROUPS):
+            finish(step, group, later)
         return carry
 
     lax.fori_loop(0, SUBSTEPS, substep, 0)
@@ -379,6 +391,14 @@
     rotation = jnp.dot(
         math.sqrt(dirs) * omega, inverse, precision=highest, preferred_element_type=jnp.float32
     )
+    mode_gram = gram_on_lat()[:, 0:dirs]
+    spread = dot_nt(
+        jnp.dot(rotation, mode_gram, precision=highest, preferred_element_type=jnp.float32),
+        rotation,
+        highest,
+    )
+    spread_ref[...] = spread * (1.0 / (fields * cells * n_lat * n_lon))
+
     c_high, c_low = split2(rotation + weights)
     for field in range(fields):
         block = pl.ds(field * cells, cells)
@@ -390,20 +410,13 @@
                 update[:, r * cols : (r + 1) * cols] + means[line : line + 1, :]
             )
 
-    mode_gram = gram_on_lat()[:, 0:dirs]
-    spread = dot_nt(
-        jnp.dot(rotation, mode_gram, precision=highest, preferred_element_type=jnp.float32),
-        rotation,
-        highest,
-    )
-    spread_ref[...] = spread * (1.0 / (fields * cells * n_lat * n_lon))
-
 
 def on_device(n_lat, n_lon, sample_collection, obs_index, obs_count, obs_value, obs_weight):
     members, fields, rows, cols = sample_collection.shape
     slots = obs_index.shape[-1]
     dirs, tiles = members - 1, members * fields
-    padded_tiles = -(-tiles // 8) * 8
+    group_tiles = -(-members // GROUPS) * fields
+    padded_tiles = -(-group_tiles // 8) * 8
     pad = -(-members // 16) * 16
     f32 = jnp.float32
     dims = (members, fields, rows, cols, n_lat, n_lon)
@@ -421,13 +434,13 @@
             pltpu.VMEM((1, slots), f32),
             pltpu.VMEM((1, slots), f32),
             pltpu.VMEM((2, tiles * rows, cols), f32),
-            pltpu.VMEM((SUBSTEPS, padded_tiles, cols), f32),
-            pltpu.VMEM((SUBSTEPS, padded_tiles, cols), f32),
-            pltpu.VMEM((SUBSTEPS, fields * rows, cols), f32),
-            pltpu.VMEM((SUBSTEPS, padded_tiles, cols), f32),
-            pltpu.VMEM((SUBSTEPS, padded_tiles, cols), f32),
-            pltpu.VMEM((SUBSTEPS, fields * rows, cols), f32),
-            pltpu.VMEM((SUBSTEPS, fields * rows, cols), f32),
+            pltpu.VMEM((SUBSTEPS, GROUPS, padded_tiles, cols), f32),
+            pltpu.VMEM((SUBSTEPS, GROUPS, padded_tiles, cols), f32),
+            pltpu.VMEM((SUBSTEPS, GROUPS, fields * rows, cols), f32),
+            pltpu.VMEM((SUBSTEPS, GROUPS, padded_tiles, cols), f32),
+            pltpu.VMEM((SUBSTEPS, GROUPS, padded_tiles, cols), f32),
+            pltpu.VMEM((SUBSTEPS, GROUPS, fields * rows, cols), f32),
+            pltpu.VMEM((SUBSTEPS, GROUPS, fields * rows, cols), f32),
             pltpu.VMEM((pad, rows * cols), f32),
             pltpu.VMEM((rows * cols, slots), jnp.bfloat16),
             pltpu.VMEM((fields * rows, cols), f32),
@@ -438,8 +451,8 @@
             pltpu.VMEM((n_lon, dirs, 128), f32),
             pltpu.VMEM((n_lat, dirs, 128), f32),
             pltpu.SemaphoreType.DMA((5,)),
-            pltpu.SemaphoreType.DMA((SUBSTEPS, 4)),
-            pltpu.SemaphoreType.DMA((SUBSTEPS, 4)),
+            pltpu.SemaphoreType.DMA((SUBSTEPS, GROUPS, 4)),
+            pltpu.SemaphoreType.DMA((SUBSTEPS, GROUPS, 4)),
         ]
         + [pltpu.SemaphoreType.DMA((n,)) for n in (n_lon, n_lon, n_lat, n_lat) * 2],
         compiler_params=pltpu.CompilerParams(

time: 37.3 us -> 36.1 us (0.968)
  Pallas kernels: 32.8 us -> 31.6 us
    pallas_call x1, Pallas kernels: 32.8 us -> 31.6 us  [on_device(): pl.pallas_call(functools.partial(kernel, dims), out_shape=(jax.ShapeDtype...]
where the time goes in v4:
time: 36.1 us; the launch traced here: 35.9 us
  Pallas kernels  31.6 us (88%)
  local copies, waits for them, and re-layouts  3.02 us (8%)
  between operations  1.31 us (4%)
    pallas_call x1, Pallas kernels, on_device(): pl.pallas_call(functools.partial(kernel, dims), out_shape=(jax.ShapeDtype...  31.6 us
    unnamed x10, local copies, waits for them, and re-layouts  3.02 us

profile of v4, /device:TPU:0, one launch (start us, length us, event | category | flops | bytes accessed | tf_op | source)
XLA Modules:
  0.0 35.9 jit_solution(13242976902419006021)
XLA Ops:
  1.3 0.0 copy-start.1
  1.3 0.0 copy-start.2
  1.3 0.0 copy-start.3
  1.3 0.6 %copy-done.1 = s32[1,1,128]{2,1,0:T(1,128)S(1)} copy-done((s32[1,1,128]{2,1,0:T(1,128)S(1)}, s32[1,1,128]{2,1,0:T(1,128)}, u32[]{:S(2)}) %copy-start.1) | copy-done | bytes 536
  1.9 0.0 copy-done.2
  1.9 0.0 copy-done.3
  2.0 0.0 copy-start
  2.0 1.0 %copy-done = f32[17,6,8,128]{3,2,1,0:T(8,128)S(1)} copy-done((f32[17,6,8,128]{3,2,1,0:T(8,128)S(1)}, f32[17,6,8,128]{3,2,1,0:T(8,128)}, u32[]{:S(2)}) %copy-start) | copy-done | bytes 417816
  3.0 31.6 %shard_map.68 = (f32[816,128]{1,0:T(8,128)S(1)}, f32[17,17]{1,0:T(8,128)S(1)}) custom-call(f32[816,128]{1,0:T(8,128)S(1)} %bitcast.5, s32[1,128]{1,0:T(1,128)S(1)} %bitcast.7, s32[1,1]{1,0:T(1,128)S(6)} %copy.9.count_hbm, f32[1,128]{1,0:T(1,128)S(1)} %bitcast.8, f32[1,128]{1,0:T(1,128)S(1)} %bitcast.9), custom_call_target="tpu_custom_call" | custom-call | tf_op jit(solution)/shard_map/pallas_call | solution.py:423
  34.6 0.8 %copy.10 = f32[17,6,8,128]{3,2,1,0:T(8,128)} copy(f32[17,6,8,128]{3,2,1,0:T(8,128)S(1)} %bitcast.6) | data formatting | bytes 835584
  35.4 0.6 %copy.11 = f32[17,17]{1,0:T(8,128)} copy(f32[17,17]{1,0:T(8,128)S(1)} %get-tuple-element.9) | data formatting | bytes 2312
Async XLA Ops:
  1.3 0.7 %copy-start.1 = (s32[1,1,128]{2,1,0:T(1,128)S(1)}, s32[1,1,128]{2,1,0:T(1,128)}, u32[]{:S(2)}) copy-start(s32[1,1,128]{2,1,0:T(1,128)} %param.6) | copy-start | bytes 1540
  1.3 0.7 %copy-start.2 = (f32[1,1,128]{2,1,0:T(1,128)S(1)}, f32[1,1,128]{2,1,0:T(1,128)}, u32[]{:S(2)}) copy-start(f32[1,1,128]{2,1,0:T(1,128)} %param.8) | copy-start | bytes 1540
  1.3 0.7 %copy-start.3 = (f32[1,1,128]{2,1,0:T(1,128)S(1)}, f32[1,1,128]{2,1,0:T(1,128)}, u32[]{:S(2)}) copy-start(f32[1,1,128]{2,1,0:T(1,128)} %param.9) | copy-start | bytes 1540
  2.0 1.0 %copy-start = (f32[17,6,8,128]{3,2,1,0:T(8,128)S(1)}, f32[17,6,8,128]{3,2,1,0:T(8,128)}, u32[]{:S(2)}) copy-start(f32[17,6,8,128]{3,2,1,0:T(8,128)} %param.5) | copy-start | bytes 1253380

commit v5 on v4

--- a/solution.py
+++ b/solution.py
@@ -22,6 +22,7 @@
 SYS = 32
 BATCH = 4
 GROUPS = 2
+VMEM_BYTES = 63 * 1024 * 1024
 
 
 def split2(x):
@@ -50,11 +51,11 @@
 
 def kernel(
     dims, x_hbm, index_hbm, count_hbm, value_hbm, weight_hbm,
-    out_ref, spread_ref,
+    out_hbm, spread_ref,
     index_ref, count_ref, value_ref, weight_ref,
-    state, send_low, send_high, send_cols, from_north, from_south, from_east, from_west,
+    out_ref, state, send_low, send_high, send_cols, from_north, from_south, from_east, from_west,
     surface, selector, means, modes, parts,
-    obs_lon, obs_lat, gram_lon, gram_lat, load_sem, halo_send, halo_recv,
+    obs_lon, obs_lat, gram_lon, gram_lat, load_sem, store_sem, halo_send, halo_recv,
     obs_lon_send, obs_lon_recv, obs_lat_send, obs_lat_recv,
     gram_lon_send, gram_lon_recv, gram_lat_send, gram_lat_recv,
 ):
@@ -112,7 +113,7 @@
 
     bounds = [members * g // GROUPS for g in range(GROUPS + 1)]
 
-    def put_edges(slot, group, now):
+    def put_cols(slot, group, now):
         first, last = bounds[group], bounds[group + 1]
         for field in range(fields):
             packed = jnp.zeros((rows, cols), jnp.float32)
@@ -122,12 +123,11 @@
                 packed = jnp.where(half == member - first, moved, packed)
             send_cols[slot, group, field * rows : (field + 1) * rows, :] = packed
         exchange_start(slot, group, "lon")
-        for tile in range(first * fields, last * fields):
-            place = slice(tile - first * fields, tile - first * fields + 1)
-            low, high = tile * rows, (tile + 1) * rows - 1
-            send_low[slot, group, place, :] = state[now, low : low + 1, :]
-            send_high[slot, group, place, :] = state[now, high : high + 1, :]
-        exchange_start(slot, group, "lat")
+
+    def lines_of(group, field, at_row):
+        first, count = bounds[group], bounds[group + 1] - bounds[group]
+        at = (first * fields + field) * rows + at_row
+        return pl.ds(at, count, stride=fields * rows), pl.ds(field, count, stride=fields)
 
     def halo_copy(step, group, number):
         source, target, device = (
@@ -179,7 +179,12 @@
         load.wait()
     pl.semaphore_wait(barrier, len(partners))
     for group in range(GROUPS):
-        put_edges(0, group, 0)
+        for sent, at_row in ((send_low, 0), (send_high, rows - 1)):
+            for field in range(fields):
+                place, line = lines_of(group, field, at_row)
+                sent[0, group, line, :] = state[0, place, :]
+        exchange_start(0, group, "lat")
+        put_cols(0, group, 0)
 
     for r in range(rows):
         cell = lax.broadcasted_iota(jnp.int32, (cols, slots), 0) + r * cols
@@ -222,17 +227,18 @@
             (from_north, send_high, rows - 1, ghost),
             (from_south, send_low, 0, -ghost),
         ):
-            lines = [pl.ds(field, last - first, stride=fields) for field in range(fields)]
+            places, lines = zip(*(lines_of(group, field, at_row) for field in range(fields)))
             halo = [source[step, group, line, :] for line in lines]
             edge = [sent[step, group, line, :] for line in lines]
             for field, added in enumerate(halo_terms(halo, edge, 2, side)):
-                at = (first * fields + field) * rows + at_row
-                place = pl.ds(at, last - first, stride=fields * rows)
-                state[later, place, :] = state[later, place, :] + added
+                moved = state[later, places[field], :] + added
+                state[later, places[field], :] = moved
+                sent[step + 1, group, lines[field], :] = moved
 
         @pl.when(step + 1 < SUBSTEPS)
         def _():
-            put_edges(step + 1, group, later)
+            exchange_start(step + 1, group, "lat")
+            put_cols(step + 1, group, later)
 
     def substep(step, carry):
         now, later = lax.rem(step, 2), lax.rem(step + 1, 2)
@@ -399,6 +405,7 @@
     )
     spread_ref[...] = spread * (1.0 / (fields * cells * n_lat * n_lon))
 
+    stores = []
     c_high, c_low = split2(rotation + weights)
     for field in range(fields):
         block = pl.ds(field * cells, cells)
@@ -406,9 +413,15 @@
         update = dot(c_high, high) + dot(c_high, parts[dirs : 2 * dirs, block]) + dot(c_low, high)
         for r in range(rows):
             line = field * rows + r
-            out_ref[pl.ds(line, members, stride=fields * rows), :] = (
-                update[:, r * cols : (r + 1) * cols] + means[line : line + 1, :]
-            )
+            out_ref[:, line, :] = update[:, r * cols : (r + 1) * cols] + means[line : line + 1, :]
+        block = slice(field * rows, (field + 1) * rows)
+        store = pltpu.make_async_copy(
+            out_ref.at[:, block, :], out_hbm.at[:, block, :], store_sem.at[field]
+        )
+        store.start()
+        stores.append(store)
+    for store in stores:
+        store.wait()
 
 
 def on_device(n_lat, n_lon, sample_collection, obs_index, obs_count, obs_value, obs_weight):
@@ -423,19 +436,23 @@
     analysis, spread = pl.pallas_call(
         functools.partial(kernel, dims),
         out_shape=(
-            jax.ShapeDtypeStruct((tiles * rows, cols), f32),
+            jax.ShapeDtypeStruct((members, fields * rows, cols), f32),
             jax.ShapeDtypeStruct((members, members), f32),
         ),
         in_specs=[pl.BlockSpec(memory_space=pltpu.HBM)] * 5,
-        out_specs=(pl.BlockSpec(memory_space=pltpu.VMEM),) * 2,
+        out_specs=(
+            pl.BlockSpec(memory_space=pltpu.HBM),
+            pl.BlockSpec(memory_space=pltpu.VMEM),
+        ),
         scratch_shapes=[
             pltpu.VMEM((1, slots), jnp.int32),
             pltpu.VMEM((1, 1), jnp.int32),
             pltpu.VMEM((1, slots), f32),
             pltpu.VMEM((1, slots), f32),
+            pltpu.VMEM((members, fields * rows, cols), f32),
             pltpu.VMEM((2, tiles * rows, cols), f32),
-            pltpu.VMEM((SUBSTEPS, GROUPS, padded_tiles, cols), f32),
-            pltpu.VMEM((SUBSTEPS, GROUPS, padded_tiles, cols), f32),
+            pltpu.VMEM((SUBSTEPS + 1, GROUPS, padded_tiles, cols), f32),
+            pltpu.VMEM((SUBSTEPS + 1, GROUPS, padded_tiles, cols), f32),
             pltpu.VMEM((SUBSTEPS, GROUPS, fields * rows, cols), f32),
             pltpu.VMEM((SUBSTEPS, GROUPS, padded_tiles, cols), f32),
             pltpu.VMEM((SUBSTEPS, GROUPS, padded_tiles, cols), f32),
@@ -451,12 +468,13 @@
             pltpu.VMEM((n_lon, dirs, 128), f32),
             pltpu.VMEM((n_lat, dirs, 128), f32),
             pltpu.SemaphoreType.DMA((5,)),
+            pltpu.SemaphoreType.DMA((fields,)),
             pltpu.SemaphoreType.DMA((SUBSTEPS, GROUPS, 4)),
             pltpu.SemaphoreType.DMA((SUBSTEPS, GROUPS, 4)),
         ]
         + [pltpu.SemaphoreType.DMA((n,)) for n in (n_lon, n_lon, n_lat, n_lat) * 2],
         compiler_params=pltpu.CompilerParams(
-            collective_id=0, has_side_effects=True, vmem_limit_bytes=32 * 1024 * 1024
+            collective_id=0, has_side_effects=True, vmem_limit_bytes=VMEM_BYTES
         ),
     )(
         sample_collection.reshape(tiles * rows, cols),

time: 36.1 us -> 36.7 us (1.017)
  Pallas kernels: 31.6 us -> 32.8 us
  local copies, waits for them, and re-layouts: 3.02 us -> 2.39 us
    pallas_call x1, Pallas kernels: 31.6 us -> 32.8 us  [on_device(): pl.pallas_call(functools.partial(kernel, dims), out_shape=(jax.ShapeDtype...]
    unnamed x10 -> x4, local copies, waits for them, and re-layouts: 3.02 us -> 2.39 us
where the time goes in v5:
time: 36.7 us; the launch traced here: 36.5 us
  Pallas kernels  32.8 us (89%)
  local copies, waits for them, and re-layouts  2.39 us (7%)
  between operations  1.29 us (4%)
    pallas_call x1, Pallas kernels, on_device(): pl.pallas_call(functools.partial(kernel, dims), out_shape=(jax.ShapeDtype...  32.8 us
    unnamed x4, local copies, waits for them, and re-layouts  2.39 us

profile of v5, /device:TPU:0, one launch (start us, length us, event | category | flops | bytes accessed | tf_op | source)
XLA Modules:
  0.0 36.5 jit_solution(9602868752457845106)
XLA Ops:
  1.3 32.8 %shard_map.68 = (f32[17,48,128]{2,1,0:T(8,128)}, f32[17,17]{1,0:T(8,128)}) custom-call(f32[816,128]{1,0:T(8,128)} %bitcast.5, s32[1,128]{1,0:T(1,128)} %bitcast.7, s32[1,1]{1,0:T(1,128)S(6)} %copy.9.count_hbm, f32[1,128]{1,0:T(1,128)} %bitcast.8, f32[1,128]{1,0:T(1,128)} %bitcast.9), custom_call_target="tpu_custom_call" | custom-call | tf_op jit(solution)/shard_map/pallas_call | solution.py:436
  34.1 0.0 copy-start
  34.1 1.8 %copy.10 = f32[17,6,8,128]{3,2,1,0:T(8,128)} copy(f32[17,6,8,128]{3,2,1,0:T(8,128)} %bitcast.6) | data formatting | bytes 835584
  35.9 0.0 copy-done
  35.9 0.6 %copy.11 = f32[17,17]{1,0:T(8,128)} copy(f32[17,17]{1,0:T(8,128)S(1)} %copy-done) | data formatting | bytes 2312
Async XLA Ops:
  34.1 1.8 %copy-start = (f32[17,17]{1,0:T(8,128)S(1)}, f32[17,17]{1,0:T(8,128)}, u32[]{:S(2)}) copy-start(f32[17,17]{1,0:T(8,128)} %get-tuple-element.9) | copy-start | bytes 3472

commit v6 on v5

--- a/solution.py
+++ b/solution.py
@@ -19,10 +19,11 @@
 highest = lax.Precision.HIGHEST
 MESH = pl.DeviceIdType.MESH
 
-SYS = 32
+COPIES = 3
+SYS = 64
 BATCH = 4
 GROUPS = 2
-VMEM_BYTES = 63 * 1024 * 1024
+VMEM_BYTES = 32 * 1024 * 1024
 
 
 def split2(x):
@@ -51,11 +52,11 @@
 
 def kernel(
     dims, x_hbm, index_hbm, count_hbm, value_hbm, weight_hbm,
-    out_hbm, spread_ref,
+    out_ref, spread_ref,
     index_ref, count_ref, value_ref, weight_ref,
-    out_ref, state, send_low, send_high, send_cols, from_north, from_south, from_east, from_west,
+    state, send_low, send_high, send_cols, from_north, from_south, from_east, from_west,
     surface, selector, means, modes, parts,
-    obs_lon, obs_lat, gram_lon, gram_lat, load_sem, store_sem, halo_send, halo_recv,
+    obs_lon, obs_lat, gram_lon, gram_lat, load_sem, halo_send, halo_recv,
     obs_lon_send, obs_lon_recv, obs_lat_send, obs_lat_recv,
     gram_lon_send, gram_lon_recv, gram_lat_send, gram_lat_recv,
 ):
@@ -356,9 +357,13 @@
         high, low = split2(modes[pl.ds(line, dirs, stride=fields * rows), :])
         parts[0:dirs, line * cols : (line + 1) * cols] = high
         parts[dirs : 2 * dirs, line * cols : (line + 1) * cols] = low
-    high, low = parts[0:dirs, :], parts[dirs : 2 * dirs, :]
+        parts[2 * dirs : 3 * dirs, line * cols : (line + 1) * cols] = high
+    both = parts[0 : 2 * dirs, :]
+    gram = dot_nt(both, both)
     gram_lon[me_lon] = jnp.zeros(gram_lon.shape[1:], jnp.float32)
-    gram_lon[me_lon, :, 0:dirs] = dot_nt(high, high) + dot_nt(high, low) + dot_nt(low, high)
+    gram_lon[me_lon, :, 0:dirs] = (
+        gram[0:dirs, 0:dirs] + gram[0:dirs, dirs : 2 * dirs] + gram[dirs : 2 * dirs, 0:dirs]
+    )
     gram_on_lon = gather(gram_lon, me_lon, n_lon, lon_at, gram_lon_send, gram_lon_recv)
 
     obs_lat[me_lat] = obs_on_lon()
@@ -368,7 +373,7 @@
 
     below = lax.broadcasted_iota(jnp.int32, (dirs, 128), 0)
     across = lax.broadcasted_iota(jnp.int32, (dirs, 128), 1)
-    identity = jnp.where(across == below, 1.0, 0.0)
+    identity = sum(jnp.where(across == below + i * dirs, 1.0, 0.0) for i in range(COPIES))
     inside = (across >= SYS) & (across < SYS + dirs)
     gamma = jnp.where(across == below + SYS, 1.0, 0.0) - jnp.where(inside, 1.0 / members, 0.0)
     system = obs_on_lat() + (identity + dirs / forget * gamma)
@@ -386,17 +391,21 @@
     diagonal = jnp.sum(jnp.where(across == below + SYS, system, 0.0), axis=1, keepdims=True)
     system = system / jnp.sqrt(diagonal)
     solved = system[:, SYS + dirs : SYS + dirs + 1]
-    inverse = system[:, 0:dirs]
+    inverse = system[:, 0 : COPIES * dirs]
     weights = jnp.sum(solved * inverse, axis=0, keepdims=True)
     shift = (math.sqrt(members) - 1.0) / dirs
-    body = (shift - 1.0) / members
-    tail = -math.sqrt(members) / members
-    place = lax.broadcasted_iota(jnp.int32, (members, dirs), 0)
-    mode = lax.broadcasted_iota(jnp.int32, (members, dirs), 1)
-    omega = jnp.where(place == dirs, tail, jnp.where(place == mode, 1.0 + body, body))
-    rotation = jnp.dot(
-        math.sqrt(dirs) * omega, inverse, precision=highest, preferred_element_type=jnp.float32
-    )
+    body = math.sqrt(dirs) * (shift - 1.0) / members
+    tail = -math.sqrt(dirs) * math.sqrt(members) / members
+    over_rows = jnp.sum(inverse, axis=0, keepdims=True)
+    rotation = jnp.concatenate(
+        [
+            math.sqrt(dirs) * inverse + body * over_rows,
+            jnp.broadcast_to(tail * over_rows, (8, COPIES * dirs)),
+        ],
+        axis=0,
+    )
+    coefficient = rotation + weights
+    rotation = rotation[0:members, 0:dirs]
     mode_gram = gram_on_lat()[:, 0:dirs]
     spread = dot_nt(
         jnp.dot(rotation, mode_gram, precision=highest, preferred_element_type=jnp.float32),
@@ -405,23 +414,14 @@
     )
     spread_ref[...] = spread * (1.0 / (fields * cells * n_lat * n_lon))
 
-    stores = []
-    c_high, c_low = split2(rotation + weights)
+    c_high = coefficient.astype(jnp.bfloat16).astype(jnp.float32)
+    part = lax.broadcasted_iota(jnp.int32, coefficient.shape, 1)
+    c_parts = jnp.where(part < 2 * dirs, c_high, coefficient - c_high).astype(jnp.bfloat16)
     for field in range(fields):
-        block = pl.ds(field * cells, cells)
-        high = parts[0:dirs, block]
-        update = dot(c_high, high) + dot(c_high, parts[dirs : 2 * dirs, block]) + dot(c_low, high)
+        update = dot(c_parts, parts[:, field * cells : (field + 1) * cells])
         for r in range(rows):
             line = field * rows + r
-            out_ref[:, line, :] = update[:, r * cols : (r + 1) * cols] + means[line : line + 1, :]
-        block = slice(field * rows, (field + 1) * rows)
-        store = pltpu.make_async_copy(
-            out_ref.at[:, block, :], out_hbm.at[:, block, :], store_sem.at[field]
-        )
-        store.start()
-        stores.append(store)
-    for store in stores:
-        store.wait()
+            out_ref[:, line, :] = update[0:members, r * cols : (r + 1) * cols] + means[line : line + 1, :]
 
 
 def on_device(n_lat, n_lon, sample_collection, obs_index, obs_count, obs_value, obs_weight):
@@ -440,16 +440,12 @@
             jax.ShapeDtypeStruct((members, members), f32),
         ),
         in_specs=[pl.BlockSpec(memory_space=pltpu.HBM)] * 5,
-        out_specs=(
-            pl.BlockSpec(memory_space=pltpu.HBM),
-            pl.BlockSpec(memory_space=pltpu.VMEM),
-        ),
+        out_specs=(pl.BlockSpec(memory_space=pltpu.VMEM),) * 2,
         scratch_shapes=[
             pltpu.VMEM((1, slots), jnp.int32),
             pltpu.VMEM((1, 1), jnp.int32),
             pltpu.VMEM((1, slots), f32),
             pltpu.VMEM((1, slots), f32),
-            pltpu.VMEM((members, fields * rows, cols), f32),
             pltpu.VMEM((2, tiles * rows, cols), f32),
             pltpu.VMEM((SUBSTEPS + 1, GROUPS, padded_tiles, cols), f32),
             pltpu.VMEM((SUBSTEPS + 1, GROUPS, padded_tiles, cols), f32),
@@ -462,13 +458,12 @@
             pltpu.VMEM((rows * cols, slots), jnp.bfloat16),
             pltpu.VMEM((fields * rows, cols), f32),
             pltpu.VMEM((dirs * fields * rows, cols), f32),
-            pltpu.VMEM((2 * dirs, fields * rows * cols), jnp.bfloat16),
+            pltpu.VMEM((COPIES * dirs, fields * rows * cols), jnp.bfloat16),
             pltpu.VMEM((n_lon, dirs, 128), f32),
             pltpu.VMEM((n_lat, dirs, 128), f32),
             pltpu.VMEM((n_lon, dirs, 128), f32),
             pltpu.VMEM((n_lat, dirs, 128), f32),
             pltpu.SemaphoreType.DMA((5,)),
-            pltpu.SemaphoreType.DMA((fields,)),
             pltpu.SemaphoreType.DMA((SUBSTEPS, GROUPS, 4)),
             pltpu.SemaphoreType.DMA((SUBSTEPS, GROUPS, 4)),
         ]

time: 36.7 us -> 35.7 us (0.973)
  Pallas kernels: 32.8 us -> 31.2 us
  local copies, waits for them, and re-layouts: 2.39 us -> 3.02 us
    pallas_call x1, Pallas kernels: 32.8 us -> 31.2 us  [on_device(): pl.pallas_call(functools.partial(kernel, dims), out_shape=(jax.ShapeDtype...]
    unnamed x4 -> x10, local copies, waits for them, and re-layouts: 2.39 us -> 3.02 us
where the time goes in v6:
time: 35.7 us; the launch traced here: 35.5 us
  Pallas kernels  31.2 us (87%)
  local copies, waits for them, and re-layouts  3.02 us (8%)
  between operations  1.31 us (4%)
    pallas_call x1, Pallas kernels, on_device(): pl.pallas_call(functools.partial(kernel, dims), out_shape=(jax.ShapeDtype...  31.2 us
    unnamed x10, local copies, waits for them, and re-layouts  3.02 us

profile of v6, /device:TPU:0, one launch (start us, length us, event | category | flops | bytes accessed | tf_op | source)
XLA Modules:
  0.0 35.5 jit_solution(4616618320740072619)
XLA Ops:
  1.3 0.0 copy-start.1
  1.3 0.0 copy-start.2
  1.3 0.0 copy-start.3
  1.3 0.6 %copy-done.1 = s32[1,1,128]{2,1,0:T(1,128)S(1)} copy-done((s32[1,1,128]{2,1,0:T(1,128)S(1)}, s32[1,1,128]{2,1,0:T(1,128)}, u32[]{:S(2)}) %copy-start.1) | copy-done | bytes 536
  1.9 0.0 copy-done.2
  1.9 0.0 copy-done.3
  2.0 0.0 copy-start
  2.0 1.0 %copy-done = f32[17,6,8,128]{3,2,1,0:T(8,128)S(1)} copy-done((f32[17,6,8,128]{3,2,1,0:T(8,128)S(1)}, f32[17,6,8,128]{3,2,1,0:T(8,128)}, u32[]{:S(2)}) %copy-start) | copy-done | bytes 417816
  3.0 31.2 %shard_map.68 = (f32[17,48,128]{2,1,0:T(8,128)S(1)}, f32[17,17]{1,0:T(8,128)S(1)}) custom-call(f32[816,128]{1,0:T(8,128)S(1)} %bitcast.5, s32[1,128]{1,0:T(1,128)S(1)} %bitcast.7, s32[1,1]{1,0:T(1,128)S(6)} %copy.9.count_hbm, f32[1,128]{1,0:T(1,128)S(1)} %bitcast.8, f32[1,128]{1,0:T(1,128)S(1)} %bitcast.9), custom_call_target="tpu_custom_call" | custom-call | tf_op jit(solution)/shard_map/pallas_call | solution.py:436
  34.2 0.8 %copy.10 = f32[17,6,8,128]{3,2,1,0:T(8,128)} copy(f32[17,6,8,128]{3,2,1,0:T(8,128)S(1)} %bitcast.6) | data formatting | bytes 835584
  34.9 0.6 %copy.11 = f32[17,17]{1,0:T(8,128)} copy(f32[17,17]{1,0:T(8,128)S(1)} %get-tuple-element.9) | data formatting | bytes 2312
Async XLA Ops:
  1.3 0.7 %copy-start.1 = (s32[1,1,128]{2,1,0:T(1,128)S(1)}, s32[1,1,128]{2,1,0:T(1,128)}, u32[]{:S(2)}) copy-start(s32[1,1,128]{2,1,0:T(1,128)} %param.6) | copy-start | bytes 1540
  1.3 0.7 %copy-start.2 = (f32[1,1,128]{2,1,0:T(1,128)S(1)}, f32[1,1,128]{2,1,0:T(1,128)}, u32[]{:S(2)}) copy-start(f32[1,1,128]{2,1,0:T(1,128)} %param.8) | copy-start | bytes 1540
  1.3 0.7 %copy-start.3 = (f32[1,1,128]{2,1,0:T(1,128)S(1)}, f32[1,1,128]{2,1,0:T(1,128)}, u32[]{:S(2)}) copy-start(f32[1,1,128]{2,1,0:T(1,128)} %param.9) | copy-start | bytes 1540
  2.0 1.0 %copy-start = (f32[17,6,8,128]{3,2,1,0:T(8,128)S(1)}, f32[17,6,8,128]{3,2,1,0:T(8,128)}, u32[]{:S(2)}) copy-start(f32[17,6,8,128]{3,2,1,0:T(8,128)} %param.5) | copy-start | bytes 1253380

commit v7 on v6

--- a/solution.py
+++ b/solution.py
@@ -54,7 +54,7 @@
     dims, x_hbm, index_hbm, count_hbm, value_hbm, weight_hbm,
     out_ref, spread_ref,
     index_ref, count_ref, value_ref, weight_ref,
-    state, send_low, send_high, send_cols, from_north, from_south, from_east, from_west,
+    state, other, send_low, send_high, send_cols, from_north, from_south, from_east, from_west,
     surface, selector, means, modes, parts,
     obs_lon, obs_lat, gram_lon, gram_lat, load_sem, halo_send, halo_recv,
     obs_lon_send, obs_lon_recv, obs_lat_send, obs_lat_recv,
@@ -81,7 +81,7 @@
     loads = [
         pltpu.make_async_copy(source, target, load_sem.at[number])
         for number, (source, target) in enumerate((
-            (x_hbm, state.at[0]),
+            (x_hbm, state),
             (index_hbm, index_ref),
             (count_hbm, count_ref),
             (value_hbm, value_ref),
@@ -120,7 +120,7 @@
             packed = jnp.zeros((rows, cols), jnp.float32)
             for member in range(first, last):
                 at = (member * fields + field) * rows
-                moved = pltpu.roll(state[now, at : at + rows, :], 2 * (member - first) + 1, 1)
+                moved = pltpu.roll(now[at : at + rows, :], 2 * (member - first) + 1, 1)
                 packed = jnp.where(half == member - first, moved, packed)
             send_cols[slot, group, field * rows : (field + 1) * rows, :] = packed
         exchange_start(slot, group, "lon")
@@ -183,9 +183,9 @@
         for sent, at_row in ((send_low, 0), (send_high, rows - 1)):
             for field in range(fields):
                 place, line = lines_of(group, field, at_row)
-                sent[0, group, line, :] = state[0, place, :]
+                sent[0, group, line, :] = state[place, :]
         exchange_start(0, group, "lat")
-        put_cols(0, group, 0)
+        put_cols(0, group, state)
 
     for r in range(rows):
         cell = lax.broadcasted_iota(jnp.int32, (cols, slots), 0) + r * cols
@@ -218,10 +218,16 @@
             edge.append(send_cols[step, group, block, :])
         side = jnp.where(even_lane, ghost, -ghost)
         for field, added in enumerate(halo_terms(halo, edge, 1, side)):
-            for member in range(first, last):
-                at = (member * fields + field) * rows
-                moved = pltpu.roll(added, cols - 1 - 2 * (member - first), 1)
-                state[later, at : at + rows, :] += jnp.where(edge_lane, moved, 0.0)
+            tiles_here = [
+                slice((member * fields + field) * rows, (member * fields + field + 1) * rows)
+                for member in range(first, last)
+            ]
+            sums = []
+            for number, place in enumerate(tiles_here):
+                moved = pltpu.roll(added, cols - 1 - 2 * number, 1)
+                sums.append(later[place, :] + jnp.where(edge_lane, moved, 0.0))
+            for place, value in zip(tiles_here, sums):
+                later[place, :] = value
 
         exchange_end(step, group, "lat")
         for source, sent, at_row, side in (
@@ -231,23 +237,25 @@
             places, lines = zip(*(lines_of(group, field, at_row) for field in range(fields)))
             halo = [source[step, group, line, :] for line in lines]
             edge = [sent[step, group, line, :] for line in lines]
-            for field, added in enumerate(halo_terms(halo, edge, 2, side)):
-                moved = state[later, places[field], :] + added
-                state[later, places[field], :] = moved
-                sent[step + 1, group, lines[field], :] = moved
+            sums = [
+                later[place, :] + added
+                for place, added in zip(places, halo_terms(halo, edge, 2, side))
+            ]
+            for place, line, value in zip(places, lines, sums):
+                later[place, :] = value
+                sent[step + 1, group, line, :] = value
 
         @pl.when(step + 1 < SUBSTEPS)
         def _():
             exchange_start(step + 1, group, "lat")
             put_cols(step + 1, group, later)
 
-    def substep(step, carry):
-        now, later = lax.rem(step, 2), lax.rem(step + 1, 2)
+    def substep(step, now, later):
         for member in range(members):
             here, east, west, north, south = [], [], [], [], []
             for field in range(fields):
                 tile = member * fields + field
-                q = state[now, tile * rows : (tile + 1) * rows, :]
+                q = now[tile * rows : (tile + 1) * rows, :]
                 here.append(q)
                 east.append(jnp.where(last_lane, 0.0, pltpu.roll(q, cols - 1, 1)))
                 west.append(jnp.where(first_lane, 0.0, pltpu.roll(q, 1, 1)))
@@ -278,14 +286,18 @@
                 )
             for field in range(fields):
                 tile = member * fields + field
-                state[later, tile * rows : (tile + 1) * rows, :] = after[field]
+                later[tile * rows : (tile + 1) * rows, :] = after[field]
 
         for group in range(GROUPS):
             finish(step, group, later)
+
+    def two_substeps(pair, carry):
+        substep(2 * pair, state, other)
+        substep(2 * pair + 1, other, state)
         return carry
 
-    lax.fori_loop(0, SUBSTEPS, substep, 0)
-    final = SUBSTEPS % 2
+
+    lax.fori_loop(0, SUBSTEPS // 2, two_substeps, 0)
 
     def gather(buffer, me, count, device_of, send, recv):
         copies = []
@@ -326,8 +338,8 @@
     for r in range(rows):
         block = slice(r * cols, (r + 1) * cols)
         surface[0:members, block] = (
-            state[final, pl.ds(r, members, stride=fields * rows), :]
-            + state[final, pl.ds(3 * rows + r, members, stride=fields * rows), :]
+            state[pl.ds(r, members, stride=fields * rows), :]
+            + state[pl.ds(3 * rows + r, members, stride=fields * rows), :]
         )
         level = jnp.concatenate(split3(surface[:, block]), axis=0)
         observed += dot(level, selector[block, :])
@@ -344,15 +356,15 @@
     obs_on_lon = gather(obs_lon, me_lon, n_lon, lon_at, obs_lon_send, obs_lon_recv)
 
     for field in range(fields):
-        total = state[final, field * rows : (field + 1) * rows, :]
+        total = state[field * rows : (field + 1) * rows, :]
         for member in range(1, members):
             at = (member * fields + field) * rows
-            total = total + state[final, at : at + rows, :]
+            total = total + state[at : at + rows, :]
         total = total * (1.0 / members)
         means[field * rows : (field + 1) * rows, :] = total
         for member in range(dirs):
             at = (member * fields + field) * rows
-            modes[at : at + rows, :] = state[final, at : at + rows, :] - total
+            modes[at : at + rows, :] = state[at : at + rows, :] - total
     for line in range(fields * rows):
         high, low = split2(modes[pl.ds(line, dirs, stride=fields * rows), :])
         parts[0:dirs, line * cols : (line + 1) * cols] = high
@@ -446,7 +458,8 @@
             pltpu.VMEM((1, 1), jnp.int32),
             pltpu.VMEM((1, slots), f32),
             pltpu.VMEM((1, slots), f32),
-            pltpu.VMEM((2, tiles * rows, cols), f32),
+            pltpu.VMEM((tiles * rows, cols), f32),
+            pltpu.VMEM((tiles * rows, cols), f32),
             pltpu.VMEM((SUBSTEPS + 1, GROUPS, padded_tiles, cols), f32),
             pltpu.VMEM((SUBSTEPS + 1, GROUPS, padded_tiles, cols), f32),
             pltpu.VMEM((SUBSTEPS, GROUPS, fields * rows, cols), f32),

time: 35.7 us -> 35.7 us (level)
  no operation moved by 1% of the time
where the time goes in v7:
time: 35.7 us; the launch traced here: 35.5 us
  Pallas kernels  31.2 us (87%)
  local copies, waits for them, and re-layouts  3.02 us (8%)
  between operations  1.31 us (4%)
    pallas_call x1, Pallas kernels, on_device(): pl.pallas_call(functools.partial(kernel, dims), out_shape=(jax.ShapeDtype...  31.2 us
    unnamed x10, local copies, waits for them, and re-layouts  3.02 us

profile of v7, /device:TPU:0, one launch (start us, length us, event | category | flops | bytes accessed | tf_op | source)
XLA Modules:
  0.0 35.5 jit_solution(14653580657083732343)
XLA Ops:
  1.3 0.0 copy-start.1
  1.3 0.0 copy-start.2
  1.3 0.0 copy-start.3
  1.3 0.6 %copy-done.1 = s32[1,1,128]{2,1,0:T(1,128)S(1)} copy-done((s32[1,1,128]{2,1,0:T(1,128)S(1)}, s32[1,1,128]{2,1,0:T(1,128)}, u32[]{:S(2)}) %copy-start.1) | copy-done | bytes 536
  1.9 0.0 copy-done.2
  1.9 0.0 copy-done.3
  2.0 0.0 copy-start
  2.0 1.0 %copy-done = f32[17,6,8,128]{3,2,1,0:T(8,128)S(1)} copy-done((f32[17,6,8,128]{3,2,1,0:T(8,128)S(1)}, f32[17,6,8,128]{3,2,1,0:T(8,128)}, u32[]{:S(2)}) %copy-start) | copy-done | bytes 417816
  3.0 31.2 %shard_map.68 = (f32[17,48,128]{2,1,0:T(8,128)S(1)}, f32[17,17]{1,0:T(8,128)S(1)}) custom-call(f32[816,128]{1,0:T(8,128)S(1)} %bitcast.5, s32[1,128]{1,0:T(1,128)S(1)} %bitcast.7, s32[1,1]{1,0:T(1,128)S(6)} %copy.9.count_hbm, f32[1,128]{1,0:T(1,128)S(1)} %bitcast.8, f32[1,128]{1,0:T(1,128)S(1)} %bitcast.9), custom_call_target="tpu_custom_call" | custom-call | tf_op jit(solution)/shard_map/pallas_call | solution.py:448
  34.2 0.8 %copy.10 = f32[17,6,8,128]{3,2,1,0:T(8,128)} copy(f32[17,6,8,128]{3,2,1,0:T(8,128)S(1)} %bitcast.6) | data formatting | bytes 835584
  34.9 0.6 %copy.11 = f32[17,17]{1,0:T(8,128)} copy(f32[17,17]{1,0:T(8,128)S(1)} %get-tuple-element.9) | data formatting | bytes 2312
Async XLA Ops:
  1.3 0.7 %copy-start.1 = (s32[1,1,128]{2,1,0:T(1,128)S(1)}, s32[1,1,128]{2,1,0:T(1,128)}, u32[]{:S(2)}) copy-start(s32[1,1,128]{2,1,0:T(1,128)} %param.6) | copy-start | bytes 1540
  1.3 0.7 %copy-start.2 = (f32[1,1,128]{2,1,0:T(1,128)S(1)}, f32[1,1,128]{2,1,0:T(1,128)}, u32[]{:S(2)}) copy-start(f32[1,1,128]{2,1,0:T(1,128)} %param.8) | copy-start | bytes 1540
  1.3 0.7 %copy-start.3 = (f32[1,1,128]{2,1,0:T(1,128)S(1)}, f32[1,1,128]{2,1,0:T(1,128)}, u32[]{:S(2)}) copy-start(f32[1,1,128]{2,1,0:T(1,128)} %param.9) | copy-start | bytes 1540
  2.0 1.0 %copy-start = (f32[17,6,8,128]{3,2,1,0:T(8,128)S(1)}, f32[17,6,8,128]{3,2,1,0:T(8,128)}, u32[]{:S(2)}) copy-start(f32[17,6,8,128]{3,2,1,0:T(8,128)} %param.5) | copy-start | bytes 1253380

commit v8 on v7

--- a/solution.py
+++ b/solution.py
@@ -162,19 +162,29 @@
 
     def exchange_end(step, group, axis):
         if axis == "lon":
-            halo_copy(step, group, 2).wait()
-            halo_copy(step, group, 3).wait()
+            halo_copy(step, group, 2).wait_recv()
+            halo_copy(step, group, 3).wait_recv()
             return
 
         @pl.when(me_lat > 0)
         def _():
+            halo_copy(step, group, 1).wait_recv()
+
+        @pl.when(me_lat < n_lat - 1)
+        def _():
+            halo_copy(step, group, 0).wait_recv()
+
+    def exchange_sent(step, group):
+        halo_copy(step, group, 2).wait_send()
+        halo_copy(step, group, 3).wait_send()
+
+        @pl.when(me_lat > 0)
+        def _():
             halo_copy(step, group, 0).wait_send()
-            halo_copy(step, group, 1).wait_recv()
 
         @pl.when(me_lat < n_lat - 1)
         def _():
             halo_copy(step, group, 1).wait_send()
-            halo_copy(step, group, 0).wait_recv()
 
     for load in loads:
         load.wait()
@@ -299,8 +309,9 @@
 
     lax.fori_loop(0, SUBSTEPS // 2, two_substeps, 0)
 
+    sent_later = []
+
     def gather(buffer, me, count, device_of, send, recv):
-        copies = []
         for d in range(1, count):
             copy = pltpu.make_async_remote_copy(
                 src_ref=buffer.at[me],
@@ -311,7 +322,7 @@
                 device_id_type=MESH,
             )
             copy.start()
-            copies.append(copy)
+            sent_later.append(copy)
 
         def total():
             for d in range(1, count):
@@ -324,8 +335,6 @@
                     device_id=device_of(d),
                     device_id_type=MESH,
                 ).wait_recv()
-            for copy in copies:
-                copy.wait_send()
             result = buffer[0]
             for i in range(1, count):
                 result = result + buffer[i]
@@ -434,6 +443,12 @@
         for r in range(rows):
             line = field * rows + r
             out_ref[:, line, :] = update[0:members, r * cols : (r + 1) * cols] + means[line : line + 1, :]
+
+    for copy in sent_later:
+        copy.wait_send()
+    for step in range(SUBSTEPS):
+        for group in range(GROUPS):
+            exchange_sent(step, group)
 
 
 def on_device(n_lat, n_lon, sample_collection, obs_index, obs_count, obs_value, obs_weight):

time: 35.7 us -> 35.8 us (level)
  no operation moved by 1% of the time
where the time goes in v8:
time: 35.8 us; the launch traced here: 35.6 us
  Pallas kernels  31.3 us (87%)
  local copies, waits for them, and re-layouts  3.02 us (8%)
  between operations  1.31 us (4%)
    pallas_call x1, Pallas kernels, on_device(): pl.pallas_call(functools.partial(kernel, dims), out_shape=(jax.ShapeDtype...  31.3 us
    unnamed x10, local copies, waits for them, and re-layouts  3.02 us

profile of v8, /device:TPU:0, one launch (start us, length us, event | category | flops | bytes accessed | tf_op | source)
XLA Modules:
  0.0 35.6 jit_solution(11205273964804074564)
XLA Ops:
  1.3 0.0 copy-start.1
  1.3 0.0 copy-start.2
  1.3 0.0 copy-start.3
  1.3 0.6 %copy-done.1 = s32[1,1,128]{2,1,0:T(1,128)S(1)} copy-done((s32[1,1,128]{2,1,0:T(1,128)S(1)}, s32[1,1,128]{2,1,0:T(1,128)}, u32[]{:S(2)}) %copy-start.1) | copy-done | bytes 536
  1.9 0.0 copy-done.2
  1.9 0.0 copy-done.3
  2.0 0.0 copy-start
  2.0 1.0 %copy-done = f32[17,6,8,128]{3,2,1,0:T(8,128)S(1)} copy-done((f32[17,6,8,128]{3,2,1,0:T(8,128)S(1)}, f32[17,6,8,128]{3,2,1,0:T(8,128)}, u32[]{:S(2)}) %copy-start) | copy-done | bytes 417816
  3.0 31.3 %shard_map.68 = (f32[17,48,128]{2,1,0:T(8,128)S(1)}, f32[17,17]{1,0:T(8,128)S(1)}) custom-call(f32[816,128]{1,0:T(8,128)S(1)} %bitcast.5, s32[1,128]{1,0:T(1,128)S(1)} %bitcast.7, s32[1,1]{1,0:T(1,128)S(6)} %copy.9.count_hbm, f32[1,128]{1,0:T(1,128)S(1)} %bitcast.8, f32[1,128]{1,0:T(1,128)S(1)} %bitcast.9), custom_call_target="tpu_custom_call" | custom-call | tf_op jit(solution)/shard_map/pallas_call | solution.py:463
  34.2 0.8 %copy.10 = f32[17,6,8,128]{3,2,1,0:T(8,128)} copy(f32[17,6,8,128]{3,2,1,0:T(8,128)S(1)} %bitcast.6) | data formatting | bytes 835584
  35.0 0.6 %copy.11 = f32[17,17]{1,0:T(8,128)} copy(f32[17,17]{1,0:T(8,128)S(1)} %get-tuple-element.9) | data formatting | bytes 2312
Async XLA Ops:
  1.3 0.7 %copy-start.1 = (s32[1,1,128]{2,1,0:T(1,128)S(1)}, s32[1,1,128]{2,1,0:T(1,128)}, u32[]{:S(2)}) copy-start(s32[1,1,128]{2,1,0:T(1,128)} %param.6) | copy-start | bytes 1540
  1.3 0.7 %copy-start.2 = (f32[1,1,128]{2,1,0:T(1,128)S(1)}, f32[1,1,128]{2,1,0:T(1,128)}, u32[]{:S(2)}) copy-start(f32[1,1,128]{2,1,0:T(1,128)} %param.8) | copy-start | bytes 1540
  1.3 0.7 %copy-start.3 = (f32[1,1,128]{2,1,0:T(1,128)S(1)}, f32[1,1,128]{2,1,0:T(1,128)}, u32[]{:S(2)}) copy-start(f32[1,1,128]{2,1,0:T(1,128)} %param.9) | copy-start | bytes 1540
  2.0 1.0 %copy-start = (f32[17,6,8,128]{3,2,1,0:T(8,128)S(1)}, f32[17,6,8,128]{3,2,1,0:T(8,128)}, u32[]{:S(2)}) copy-start(f32[17,6,8,128]{3,2,1,0:T(8,128)} %param.5) | copy-start | bytes 1253380
